TPU v7x, 256 devices: a whole 4x4x8 slice. The times are simulated.
256 devices in a mesh: ctx: 16 (over x, z_hi), tp: 16 (over y, z_lo, core).
Axes of the slice: x: 4, y: 4, z: 8 (z_hi: 4, z_lo: 2; z = z_hi * 2 + z_lo), core: 2. Of those that a mesh axis runs over, the one named last changes fastest.
Arguments:
- tokens: bfloat16 [4096, 8192], P('ctx', 'tp'), may hold values from -6 to 6
- in_weight: bfloat16 [8192, 8192], P('ctx', 'tp'), may hold values from -0.09375 to 0.09375
- filters: float32 [4096, 8192], P('ctx', 'tp'), may hold values from -1 to 1
- gate: bfloat16 [4096, 8192], P('ctx', 'tp'), may hold values from -6 to 6
- cotangent: bfloat16 [4096, 8192], P('ctx', 'tp'), may hold values from -6 to 6
Outputs:
- gated_output: bfloat16 [4096, 8192], P('ctx', 'tp')
- grad_gate: bfloat16 [4096, 8192], P('ctx', 'tp')
- grad_tokens: bfloat16 [4096, 8192], P('ctx', 'tp')
All inputs are finite; a program needn't handle non-finite values.
Results may differ from a plain program's by a relative error of at most 0.028.
Values may be sent and summed in bfloat16 or wider, within the bound.
A program may use at most 128 MiB of HBM per device.

v0:
```python
import math

import jax
import jax.numpy as jnp
from jax import lax
from jax.sharding import PartitionSpec as P

PRECISE = lax.Precision.HIGHEST
TWO_PI = 2.0 * math.pi


def shortened(shard):
    return jax.tree.map(lambda a: a.astype(jnp.bfloat16) if a.dtype == jnp.float32 else a, shard)


def counting(length):
    return jnp.arange(length, dtype=jnp.int32)


def phase_table(left_index, right_index, modulus):
    product = left_index * right_index % modulus
    return product.astype(jnp.float32) * (TWO_PI / modulus)


def first_forward(pieces, offsets, blocks, total_length):
    freq_count = 2 * blocks
    angles = phase_table(counting(freq_count)[:, None], counting(blocks)[None, :], freq_count)
    real_part = jnp.einsum("kp,bpsc->bksc", jnp.cos(angles), pieces, precision=PRECISE)
    imag_part = -jnp.einsum("kp,bpsc->bksc", jnp.sin(angles), pieces, precision=PRECISE)
    twiddle = phase_table(counting(freq_count)[:, None], offsets[None, :], total_length)
    cos_twiddle = jnp.cos(twiddle)[None, :, :, None]
    sin_twiddle = jnp.sin(twiddle)[None, :, :, None]
    return jnp.stack(
        [
            real_part * cos_twiddle + imag_part * sin_twiddle,
            imag_part * cos_twiddle - real_part * sin_twiddle,
        ]
    )


def second_forward(mixture):
    length = mixture.shape[3]
    angles = phase_table(counting(length)[:, None], counting(length)[None, :], length)
    cos_table = jnp.cos(angles)
    sin_table = jnp.sin(angles)
    real_part = jnp.einsum("qr,bjrc->bjqc", cos_table, mixture[0], precision=PRECISE) + jnp.einsum(
        "qr,bjrc->bjqc", sin_table, mixture[1], precision=PRECISE
    )
    imag_part = jnp.einsum("qr,bjrc->bjqc", cos_table, mixture[1], precision=PRECISE) - jnp.einsum(
        "qr,bjrc->bjqc", sin_table, mixture[0], precision=PRECISE
    )
    return jnp.stack([real_part, imag_part])


def first_inverse(spectrum):
    length = spectrum.shape[3]
    angles = phase_table(counting(length)[:, None], counting(length)[None, :], length)
    cos_table = jnp.cos(angles)
    sin_table = jnp.sin(angles)
    real_part = jnp.einsum("rq,bjqc->bjrc", cos_table, spectrum[0], precision=PRECISE) - jnp.einsum(
        "rq,bjqc->bjrc", sin_table, spectrum[1], precision=PRECISE
    )
    imag_part = jnp.einsum("rq,bjqc->bjrc", cos_table, spectrum[1], precision=PRECISE) + jnp.einsum(
        "rq,bjqc->bjrc", sin_table, spectrum[0], precision=PRECISE
    )
    return jnp.stack([real_part, imag_part])


def turn_inverse(signal, freq_index, total_length):
    length = signal.shape[3]
    twiddle = phase_table(freq_index[:, None], counting(length)[None, :], total_length)
    cos_twiddle = jnp.cos(twiddle)[None, :, :, None]
    sin_twiddle = jnp.sin(twiddle)[None, :, :, None]
    return jnp.stack(
        [
            signal[0] * cos_twiddle - signal[1] * sin_twiddle,
            signal[1] * cos_twiddle + signal[0] * sin_twiddle,
        ]
    )


def second_inverse(mixture, blocks, total_length):
    freq_count = 2 * blocks
    angles = phase_table(counting(blocks)[:, None], counting(freq_count)[None, :], freq_count)
    real_sum = jnp.einsum(
        "pk,bksc->bpsc", jnp.cos(angles), mixture[0], precision=PRECISE
    ) - jnp.einsum("pk,bksc->bpsc", jnp.sin(angles), mixture[1], precision=PRECISE)
    return real_sum / total_length


def local_forward(signal, blocks):
    batch_count, length, channel_count = signal.shape
    share_rows = length // blocks
    pieces = signal.reshape(batch_count, blocks, share_rows, channel_count)
    mixture = first_forward(pieces, counting(share_rows), blocks, 2 * length)
    return second_forward(mixture)


def local_inverse(spectrum, blocks):
    share_rows = spectrum.shape[3]
    total_length = 2 * blocks * share_rows
    turned = turn_inverse(first_inverse(spectrum), counting(2 * blocks), total_length)
    signal = second_inverse(turned, blocks, total_length)
    return signal.reshape(signal.shape[0], blocks * share_rows, signal.shape[3])


def complex_product(spectrum, filter_real, filter_imag):
    return jnp.stack(
        [
            spectrum[0] * filter_real - spectrum[1] * filter_imag,
            spectrum[0] * filter_imag + spectrum[1] * filter_real,
        ]
    )


def per_device(tokens, in_weight, filters, gate, cotangent):
    full_rows = lax.all_gather(tokens, "tp", axis=1, tiled=True)
    weight_all = lax.all_gather(in_weight, "ctx", axis=0, tiled=True)
    values = jnp.dot(full_rows, weight_all, preferred_element_type=jnp.float32).astype(jnp.bfloat16)
    gate_wide = gate.astype(jnp.float32)
    cotangent_wide = cotangent.astype(jnp.float32)
    grad_conv = cotangent_wide * gate_wide
    signals = values.astype(jnp.float32)
    blocks = lax.axis_size("ctx")
    channel_rows = lax.all_to_all(
        jnp.stack([filters, signals, grad_conv]).astype(jnp.bfloat16),
        "ctx",
        split_axis=2,
        concat_axis=1,
        tiled=True,
    ).astype(jnp.float32)
    spectrum = local_forward(channel_rows, blocks)
    filter_real = spectrum[0, 0:1]
    filter_imag = spectrum[1, 0:1]
    pair_real = jnp.concatenate([filter_real, filter_real], axis=0)
    pair_imag = jnp.concatenate([filter_imag, -filter_imag], axis=0)
    result = local_inverse(complex_product(spectrum[:, 1:], pair_real, pair_imag), blocks)
    result = lax.all_to_all(
        shortened(result), "ctx", split_axis=1, concat_axis=2, tiled=True
    ).astype(result.dtype)
    convolved = result[0]
    grad_signal = result[1]
    gated_output = (gate_wide * convolved).astype(jnp.bfloat16)
    grad_gate = (cotangent_wide * convolved).astype(jnp.bfloat16)
    grad_values = grad_signal.astype(jnp.bfloat16)
    partial_value = lax.dot_general(
        grad_values, weight_all, (((1,), (1,)), ((), ())), preferred_element_type=jnp.float32
    )
    grad_tokens = lax.psum_scatter(
        partial_value.astype(jnp.bfloat16), "tp", scatter_dimension=1, tiled=True
    )
    return (gated_output, grad_gate, grad_tokens)


def solution(mesh):
    placed = (P("ctx", "tp"), P("ctx", "tp"), P("ctx", "tp"), P("ctx", "tp"), P("ctx", "tp"))
    return jax.shard_map(
        per_device,
        mesh=mesh,
        in_specs=placed,
        out_specs=(P("ctx", "tp"), P("ctx", "tp"), P("ctx", "tp")),
        check_vma=False,
    )
```

profile of v0, /device:TPU:1, one launch (start us, length us, event | category | flops | bytes accessed | tf_op | source)
XLA Modules:
  0.0 369.5 jit_solution(15555545594756579511)
XLA Ops:
  7.2 0.7 all-gather.3.cloned.1.call-update
  7.9 0.7 all-gather.5.cloned.1.call-update
  8.6 1.3 fusion.47
  9.9 44.1 %all-gather.3.cloned.1.call-done = bf16[256,8192]{1,0:T(8,128)(2,1)} async-done(((bf16[256,512]{1,0:T(8,128)(2,1)}), bf16[256,8192]{1,0:T(8,128)(2,1)}) %all-gather.3.cloned.1.call-update) | async-done | bytes 4194320 | tf_op jit(solution)/shard_map/all_gather | solution.py:117
  54.0 113.0 %all-gather.5.cloned.1.call-done = bf16[8192,512]{1,0:T(8,128)(2,1)} async-done(((bf16[512,512]{1,0:T(8,128)(2,1)}), bf16[8192,512]{1,0:T(8,128)(2,1)}) %all-gather.5.cloned.1.call-update) | async-done | bytes 8388624 | tf_op jit(solution)/shard_map/all_gather | solution.py:118
  167.0 7.0 %fusion.34 = bf16[1,256,512]{2,1,0:T(8,128)(2,1)S(1)} fusion(bf16[256,8192]{1,0:T(8,128)(2,1)} %all-gather.3.cloned.1.call-done, bf16[8192,512]{1,0:T(8,128)(2,1)} %all-gather.5.cloned.1.call-done), kind=kOutput, calls=%fused_computation.38 | convolution fusion | flops 2147614720 | bytes 12845056 | tf_op jit(solution)/shard_map/dot_general | solution.py:119
  174.1 1.4 copy.27
  175.5 12.0 %all-to-all-start = ((bf16[3,256,512]{1,0,2:T(4,128)(2,1)}), bf16[3,256,512]{1,0,2:T(4,128)(2,1)S(1)}, u32[]{:S(2)}, u32[]{:S(2)}) async-start(bf16[3,256,512]{1,0,2:T(4,128)(2,1)} %copy.27), calls=%async_computation | async-start | bytes 2097152 | tf_op jit(solution)/shard_map/all_to_all | solution.py:125
  187.9 26.7 %all-to-all-done = bf16[3,256,512]{1,0,2:T(4,128)(2,1)S(1)} async-done(((bf16[3,256,512]{1,0,2:T(4,128)(2,1)}), bf16[3,256,512]{1,0,2:T(4,128)(2,1)S(1)}, u32[]{:S(2)}, u32[]{:S(2)}) %all-to-all-start) | async-done | bytes 786464 | tf_op jit(solution)/shard_map/all_to_all | solution.py:125
  214.5 1.9 fusion.35
  216.5 2.6 fusion
  219.1 5.5 %fusion.2 = f32[3,32,32,256]{3,2,1,0:T(8,128)S(1)} fusion(f32[3,32,256,32]{2,1,3,0:T(8,128)S(1)} %get-tuple-element.6), kind=kOutput, calls=%fused_computation.9 | convolution fusion | flops 2416836608 | bytes 6291456 | tf_op jit(solution)/shard_map/qr,bjrc->bjqc/dot_general | solution.py:49
  224.5 5.7 %fusion.4 = f32[3,32,32,256]{3,2,1,0:T(8,128)S(1)} fusion(f32[3,32,256,32]{2,1,3,0:T(8,128)S(1)} %get-tuple-element.6), kind=kOutput, calls=%fused_computation.11 | convolution fusion | flops 2416836608 | bytes 6291456 | tf_op jit(solution)/shard_map/qr,bjrc->bjqc/dot_general | solution.py:46
  230.2 5.5 %subtract_bitcast_fusion = f32[1,3,32,256,32]{3,4,2,1,0:T(8,128)S(1)} fusion(f32[3,32,32,256]{3,2,1,0:T(8,128)S(1)} %fusion.2, f32[3,32,256,32]{2,1,3,0:T(8,128)S(1)} %get-tuple-element.5), kind=kOutput, calls=%fused_computation.7 | convolution fusion | flops 2417623040 | bytes 9437184 | tf_op jit(solution)/shard_map/qr,bjrc->bjqc/dot_general | solution.py:49
  235.9 5.7 %add_bitcast_fusion = f32[1,3,32,256,32]{3,4,2,1,0:T(8,128)S(1)} fusion(f32[3,32,32,256]{3,2,1,0:T(8,128)S(1)} %fusion.4, f32[3,32,256,32]{2,1,3,0:T(8,128)S(1)} %get-tuple-element.5), kind=kOutput, calls=%fused_computation.8 | convolution fusion | flops 2417623040 | bytes 9437184 | tf_op jit(solution)/shard_map/qr,bjrc->bjqc/dot_general | solution.py:46
  241.7 1.3 fusion.13
  243.1 2.9 fusion.52
  245.9 2.8 fusion.54
  248.8 2.9 convolution_add_fusion
  251.7 3.4 subtract_bitcast_fusion.1
  255.1 2.4 fusion.14
  257.5 2.5 fusion.31
  260.0 1.3 copy.50
  261.3 2.0 reshape.76
  263.3 22.3 %all_to_all.24 = bf16[16,2,8192]{2,1,0:T(2,128)(2,1)S(1)} all-to-all(bf16[16,2,8192]{2,1,0:T(2,128)(2,1)S(1)} %reshape.76), channel_id=1, replica_groups=mesh['ctx'=16,'tp'=16] {'ctx'}, dimensions={0} | all-to-all | bytes 1048576 | tf_op jit(solution)/shard_map/all_to_all | solution.py:138
  285.6 1.0 reshape.77
  286.7 1.2 copy.51
  288.1 7.8 %convolution_convert_fusion = bf16[256,8192]{1,0:T(8,128)(2,1)} fusion(bf16[256,512]{0,1:T(8,128)(2,1)S(1)} %bitcast.127, bf16[8192,512]{1,0:T(8,128)(2,1)} %all-gather.5.cloned.1.call-done), kind=kOutput, calls=%fused_computation | convolution fusion | flops 2149580800 | bytes 12845056 | tf_op jit(solution)/shard_map/dot_general | solution.py:146
  295.9 0.3 copy.38
  296.4 0.4 copy-done
  296.9 0.9 fusion.43
  297.8 65.0 %reduce-scatter.2.cloned.1.call-done = bf16[256,512]{1,0:T(8,128)(2,1)} async-done(((bf16[256,8192]{1,0:T(8,128)(2,1)}), bf16[256,512]{1,0:T(8,128)(2,1)}) %reduce-scatter.2.cloned.1.call-update) | async-done | bytes 262160 | tf_op jit(solution)/shard_map/reduce_scatter | solution.py:149
  (15 shorter events, 1.3 us)
Async XLA Ops:
  7.2 46.8 %all-gather.3.cloned.1.call-start = ((), (), s32[]{:S(2)}) async-start(), calls=%async_computation.3 | async-start | bytes 4456448 | tf_op jit(solution)/shard_map/all_gather | solution.py:117
  7.9 159.1 %all-gather.5.cloned.1.call-start = ((), (), s32[]{:S(2)}) async-start(), calls=%async_computation.4 | async-start | bytes 8912896 | tf_op jit(solution)/shard_map/all_gather | solution.py:118
  175.5 39.1 %all-to-all-start = ((bf16[3,256,512]{1,0,2:T(4,128)(2,1)}), bf16[3,256,512]{1,0,2:T(4,128)(2,1)S(1)}, u32[]{:S(2)}, u32[]{:S(2)}) async-start(bf16[3,256,512]{1,0,2:T(4,128)(2,1)} %copy.27), calls=%async_computation | async-start | bytes 2097152 | tf_op jit(solution)/shard_map/all_to_all | solution.py:125
  187.5 175.3 %reduce-scatter.2.cloned.1.call-start = ((), (), s32[]{:S(2)}) async-start(), calls=%async_computation.5 | async-start | bytes 4456448 | tf_op jit(solution)/shard_map/reduce_scatter | solution.py:149
  295.8 0.9 copy-start
  295.8 1.0 copy-start.1
Sparse Core Ops, SparseCore 0:
  9.8 44.1 all-gather.2
  56.4 110.5 all-gather.4
  296.0 66.7 reduce-scatter.1
where the time goes:
time: 374 us; the launch traced here: 370 us
  waiting for transfers between devices  250 us (67%)
  matrix products  58.4 us (16%)
  blocking collectives  22.3 us (6%)
  between operations  14.2 us (4%)
  starting transfers between devices  12.3 us (3%)
  local copies, waits for them, and re-layouts  8.2 us (2%)
  other arithmetic  3.94 us (1%)
    all_gather x1, waiting for transfers between devices, per_device(): weight_all = lax.all_gather(in_weight, 'ctx', axis=0, tiled=True)  113 us
    reduce_scatter x1, waiting for transfers between devices, per_device(): lax.psum_scatter(partial_value.astype(jnp.bfloat16), 'tp', scatter_dimens...  65 us
    all_gather x1, waiting for transfers between devices, per_device(): full_rows = lax.all_gather(tokens, 'tp', axis=1, tiled=True)  44.1 us
    all_to_all x1, waiting for transfers between devices, per_device(): lax.all_to_all(jnp.stack([filters, signals, grad_conv]).astype(jnp.bfloat...  26.7 us
    all_to_all x1, blocking collectives, per_device(): lax.all_to_all(shortened(result), 'ctx', split_axis=1, concat_axis=2, til...  22.3 us
    all_to_all x1, starting transfers between devices, per_device(): lax.all_to_all(jnp.stack([filters, signals, grad_conv]).astype(jnp.bfloat...  12 us
    dot_general x1, matrix products, per_device(): lax.dot_general(grad_values, weight_all, (((1,), (1,)), ((), ())), prefer...  7.76 us
  transfers between devices with their start and end apart: 4, of which 4 were waited for; matrix products, arithmetic and copies ran while one was open for 1% of the time, Pallas kernels for 0%

commit v1 on v0

v1 whole, which is shorter than its diff:
```python
import functools
import math

import jax
import jax.numpy as jnp
import numpy as np
from jax import lax
from jax.experimental import pallas as pl
from jax.experimental.pallas import tpu as pltpu
from jax.sharding import PartitionSpec as P

MESH = pl.DeviceIdType.MESH
F32 = jnp.float32
BF16 = jnp.bfloat16
TWO_PI = 2.0 * math.pi

XN, HN, YN = 4, 4, 4
GROUP = XN * HN
ROWS = 256
WIDE = 512
CH = WIDE // GROUP
HALF = GROUP + 1
ZROWS = HALF * CH
EXCH = 4
EROWS = WIDE // EXCH
ORDER = (0, 1, 3, 2)

A_F, A_G, A_GV, A_V, A_C = range(5)


def _add(a, b):
    if a is None:
        return b
    return a if b is None else a + b


def _sub(a, b):
    if b is None:
        return a
    return -b if a is None else a - b


def _turn(value, angle):
    re, im = value
    if re is None and im is None:
        return value
    quarter = angle / (math.pi / 2)
    if abs(quarter - round(quarter)) < 1e-9:
        q = round(quarter) % 4
        neg = lambda v: None if v is None else -v
        return [(re, im), (neg(im), re), (neg(re), neg(im)), (im, neg(re))][q]
    c, s = float(math.cos(angle)), float(math.sin(angle))
    mul = lambda v, f: None if v is None else v * f
    return _sub(mul(re, c), mul(im, s)), _add(mul(re, s), mul(im, c))


def _dft(values, sign):
    n = len(values)
    if n == 1:
        return values
    even, odd = _dft(values[0::2], sign), _dft(values[1::2], sign)
    out = [None] * n
    for k in range(n // 2):
        t = _turn(odd[k], sign * TWO_PI * k / n)
        out[k] = (_add(even[k][0], t[0]), _add(even[k][1], t[1]))
        out[k + n // 2] = (_sub(even[k][0], t[0]), _sub(even[k][1], t[1]))
    return out


def _pieces_forward(xs):
    even = _dft([(v, None) for v in xs], -1)
    odd = _dft([_turn((v, None), -TWO_PI * p / 32) for p, v in enumerate(xs)], -1)
    out = []
    for k in range(HALF):
        out.append(even[k // 2] if k % 2 == 0 else odd[k // 2])
    return out


def _pieces_inverse(zs):
    first = [(zs[0][0] * 0.5, None)] + [zs[2 * m] for m in range(1, 8)] + [(None, None)] * 8
    second = [zs[2 * m + 1] for m in range(8)] + [(None, None)] * 8
    even, odd = _dft(first, 1), _dft(second, 1)
    last = zs[16][0] * 0.5
    out = []
    for p in range(GROUP):
        turned = _turn(odd[p], TWO_PI * p / 32)[0]
        total = _add(even[p][0], turned)
        out.append(total + last if p % 2 == 0 else total - last)
    return out


def _tables():
    s = np.arange(ROWS, dtype=np.int64)
    angle = (s[:, None] * s[None, :] % ROWS) * (TWO_PI / ROWS)
    cos, sin = np.cos(angle), np.sin(angle)
    forward = np.block([[cos, -sin], [sin, cos]])
    inverse = forward.T / 4096.0
    k = np.arange(HALF)
    turn = (k[:, None] * s[None, :]) * (TWO_PI / 8192)
    twist = np.concatenate([np.cos(turn), np.sin(turn)], axis=1)
    twist = np.concatenate([twist, np.zeros((24 - HALF, 2 * ROWS))], axis=0)
    split = lambda m: np.stack([m.astype(jnp.bfloat16), (m - m.astype(jnp.bfloat16).astype(np.float64)).astype(jnp.bfloat16)])
    return split(forward), split(inverse), twist.astype(np.float32)


def _kernel(x_ref, w_ref, f_ref, gate_ref, cot_ref, fwd_ref, inv_ref, tw_ref,
            out_ref, gg_ref, gt_ref,
            wg, xg, ft, gt, fr, gr, vt, vr, gvs, gvr, cs, cr,
            zhi, zlo, spec_f, spec, vacc, dsh, dex, dsum, dy, tz, dz,
            s_a2a, r_a2a, s_w, r_w, s_e, r_e, s_w1, r_w1, s_xz, r_xz, s_xy, r_xy, s_xc, r_xc,
            s_dc, r_dc, s_dy, r_dy, s_dz, r_dz, l_w):
    i = lax.axis_index("ctx")
    j = lax.axis_index("tp")
    x, zh = i // HN, i % HN
    pair, h = zh // 2, zh % 2
    y, zl, c = j // 4, (j // 2) % 2, j % 2
    a = (c + h) % 2

    def dev(x=x, zh=zh, y=y, zl=zl, c=c):
        return (x * HN + zh, y * 4 + zl * 2 + c)

    def remote(src, dst, ssem, rsem, target):
        return pltpu.make_async_remote_copy(
            src_ref=src, dst_ref=dst, send_sem=ssem, recv_sem=rsem, device_id=target, device_id_type=MESH)

    barrier = pltpu.get_barrier_semaphore()

    def greet(target):
        pl.semaphore_signal(barrier, inc=1, device_id=target, device_id_type=MESH)

    def greet_ctx(o, carry):
        greet(((i + o) % GROUP, j))
        return carry

    lax.fori_loop(1, GROUP, greet_ctx, 0)
    for o in (1, 2, 3):
        greet(dev(y=(y + o) % YN))
    greet(dev(c=1 - c))
    greet(dev(zh=2 * pair, zl=1 - zl))
    greet(dev(zh=2 * pair + 1, zl=1 - zl))
    pl.semaphore_wait(barrier, GROUP - 1 + 3 + 1 + 2)

    def spread(kind, src_of, dst, own):
        def step(o, carry):
            g = (i + o) % GROUP
            remote(src_of(g), dst, s_a2a.at[kind, g], r_a2a.at[kind, i], (g, j)).start()
            return carry
        lax.fori_loop(1, GROUP, step, 0)
        own()

    def arrive(kind, dst_of, src):
        def step(o, carry):
            g = (i + o) % GROUP
            remote(src, dst_of(g), s_a2a.at[kind, g], r_a2a.at[kind, g], (g, j)).wait_recv()
            return carry
        lax.fori_loop(1, GROUP, step, 0)

    def sent(kind, src):
        def step(o, carry):
            g = (i + o) % GROUP
            remote(src, src, s_a2a.at[kind, g], r_a2a.at[kind, g], (g, j)).wait_send()
            return carry
        lax.fori_loop(1, GROUP, step, 0)

    def rows32(g):
        return pl.ds(pl.multiple_of(g * CH, CH), CH)

    zh_d = 2 * pair + (c + zl + pair) % 2
    t_d = (zl + pair) % 2
    myrows = pl.ds(pl.multiple_of(h * ROWS, ROWS), ROWS)
    here = zh_d == zh

    def xz_copy(which):
        target = dev(zh=zh_d, zl=zl if which == 0 else 1 - zl)
        return remote(x_ref, xg.at[t_d, y, myrows], s_xz.at[which], r_xz.at[h], target)

    xz_copy(1).start()

    @pl.when(jnp.logical_not(here))
    def _():
        xz_copy(0).start()

    @pl.when(here)
    def _():
        xg[t_d, y, myrows] = x_ref[...]

    def w_copy(o):
        return remote(w_ref, wg.at[0, x], s_w.at[o], r_w.at[x], dev(x=(x + o) % XN))

    def e_copy(k):
        part = pl.ds(k * EROWS, EROWS)
        return remote(w_ref.at[part], wg.at[1, x, part], s_e.at[k], r_e.at[k], dev(zh=3 - zh))

    w_local = pltpu.make_async_copy(w_ref, wg.at[0, x], l_w.at[0])
    w_local.start()
    for o in ORDER[1:]:
        w_copy(o).start()

    ft[...] = jnp.transpose(f_ref[...]).astype(BF16)

    def own_f():
        fr[i] = ft[rows32(i), :]

    spread(A_F, lambda g: ft.at[rows32(g)], fr.at[i], own_f)
    gt[...] = jnp.transpose(cot_ref[...].astype(F32) * gate_ref[...].astype(F32)).astype(BF16)

    def own_g():
        gr[i] = gt[rows32(i), :]

    spread(A_G, lambda g: gt.at[rows32(g)], gr.at[i], own_g)
    for k in range(EXCH):
        e_copy(k).start()

    def to_spectrum(load, out):
        def step(it, carry):
            c0 = pl.multiple_of((it // 2) * 16, 16)
            l0 = pl.multiple_of((it % 2) * 128, 128)
            zs = _pieces_forward([load(p, c0, l0) for p in range(GROUP)])
            for k in range(HALF):
                re, im = zs[k]
                if k > 0:
                    co = tw_ref[k:k + 1, pl.ds(l0, 128)]
                    si = tw_ref[k:k + 1, pl.ds(l0 + ROWS, 128)]
                    if im is None:
                        re, im = re * co, -(re * si)
                    else:
                        re, im = re * co + im * si, im * co - re * si
                if im is None:
                    im = jnp.zeros_like(re)
                at = pl.ds(pl.multiple_of(k * CH + c0, 16), 16)
                for part, off in ((re, 0), (im, ROWS)):
                    hi = part.astype(BF16)
                    zhi[at, pl.ds(l0 + off, 128)] = hi
                    zlo[at, pl.ds(l0 + off, 128)] = (part - hi.astype(F32)).astype(BF16)
            return carry
        lax.fori_loop(0, 4, step, 0)
        out[...] = (jnp.dot(zhi[...], fwd_ref[0], preferred_element_type=F32)
                    + jnp.dot(zlo[...], fwd_ref[0], preferred_element_type=F32)
                    + jnp.dot(zhi[...], fwd_ref[1], preferred_element_type=F32))

    def from_spectrum(sign, store):
        def product(k, carry):
            at = pl.ds(pl.multiple_of(k * CH, CH), CH)
            ar, ai = spec[at, :ROWS], spec[at, ROWS:]
            br, bi = spec_f[at, :ROWS], spec_f[at, ROWS:]
            if sign > 0:
                re, im = ar * br - ai * bi, ar * bi + ai * br
            else:
                re, im = ar * br + ai * bi, ai * br - ar * bi
            hr_, hi_ = re.astype(BF16), im.astype(BF16)
            zhi[at, :ROWS] = hr_
            zhi[at, ROWS:] = hi_
            zlo[at, :ROWS] = (re - hr_.astype(F32)).astype(BF16)
            zlo[at, ROWS:] = (im - hi_.astype(F32)).astype(BF16)
            return carry
        lax.fori_loop(0, HALF, product, 0)
        spec[...] = (jnp.dot(zhi[...], inv_ref[0], preferred_element_type=F32)
                     + jnp.dot(zlo[...], inv_ref[0], preferred_element_type=F32)
                     + jnp.dot(zhi[...], inv_ref[1], preferred_element_type=F32))

        def step(it, carry):
            c0 = pl.multiple_of((it // 2) * 16, 16)
            l0 = pl.multiple_of((it % 2) * 128, 128)
            zs = []
            for k in range(HALF):
                at = pl.ds(pl.multiple_of(k * CH + c0, 16), 16)
                re, im = spec[at, pl.ds(l0, 128)], spec[at, pl.ds(l0 + ROWS, 128)]
                if k > 0:
                    co = tw_ref[k:k + 1, pl.ds(l0, 128)]
                    si = tw_ref[k:k + 1, pl.ds(l0 + ROWS, 128)]
                    re, im = re * co - im * si, im * co + re * si
                zs.append((re, im))
            for p, v in enumerate(_pieces_inverse(zs)):
                store(p, c0, l0, v.astype(BF16))
            return carry
        lax.fori_loop(0, 4, step, 0)

    zl_s = (c + h + pair) % 2
    mine = jnp.logical_and(zl_s == zl, True)

    def xz_wait(hr):
        remote(x_ref, xg.at[a, y, pl.ds(hr * ROWS, ROWS)], s_xz.at[0], r_xz.at[hr], dev(c=1 - c)).wait_recv()

    for hr in (0, 1):
        @pl.when(jnp.logical_not(jnp.logical_and(hr == h, zl_s == zl)))
        def _(hr=hr):
            xz_wait(hr)

    def xy_copy(o):
        return remote(xg.at[a, y], xg.at[a, y], s_xy.at[o], r_xy.at[y], dev(y=(y + o) % YN))

    def xc_copy(yy):
        return remote(xg.at[a, yy], xg.at[a, yy], s_xc.at[yy], r_xc.at[yy], dev(c=1 - c))

    for o in ORDER[1:]:
        xy_copy(o).start()
    xc_copy(y).start()

    arrive(A_F, lambda g: fr.at[g], ft.at[rows32(0)])
    to_spectrum(lambda p, c0, l0: fr[p, pl.ds(c0, 16), pl.ds(l0, 128)].astype(F32), spec_f)
    arrive(A_G, lambda g: gr.at[g], gt.at[rows32(0)])
    to_spectrum(lambda p, c0, l0: gr[p, pl.ds(c0, 16), pl.ds(l0, 128)].astype(F32), spec)

    def store_gv(p, c0, l0, v):
        gvs[p // 2, pl.ds(c0, 16), pl.ds((p % 2) * ROWS + l0, 128)] = v

    from_spectrum(-1, store_gv)

    def own_gv():
        gvr[rows32(i), :] = gvs[i // 2]

    spread(A_GV, lambda g: gvs.at[g // 2], gvr.at[rows32(i)], own_gv)

    def w1_copy(k, o):
        part = pl.ds(k * EROWS, EROWS)
        return remote(wg.at[1, x, part], wg.at[1, x, part], s_w1.at[k, o], r_w1.at[k, x], dev(x=(x + o) % XN))

    for k in range(EXCH):
        e_copy(k).wait_recv()
        for o in ORDER[1:]:
            w1_copy(k, o).start()

    for o in ORDER[1:]:
        yy = (y + o) % YN
        remote(xg.at[a, y], xg.at[a, yy], s_xy.at[o], r_xy.at[yy], dev(c=1 - c)).wait_recv()
        xc_copy(yy).start()

    for yy in range(YN):
        remote(xg.at[a, yy], xg.at[1 - a, yy], s_xc.at[yy], r_xc.at[yy], dev(c=1 - c)).wait_recv()

    w_local.wait()

    def w_wait(o):
        xx = (x + o) % XN
        remote(w_ref, wg.at[0, xx], s_w.at[o], r_w.at[xx], dev(c=1 - c)).wait_recv()

    def w1_wait(o):
        xx = (x + o) % XN
        for k in range(EXCH):
            part = pl.ds(k * EROWS, EROWS)
            remote(w_ref.at[part], wg.at[1, xx, part], s_w1.at[k, o], r_w1.at[k, xx], dev(c=1 - c)).wait_recv()

    def value_term(t, xx, first):
        term = jnp.dot(xg[t, xx], wg[t, xx], preferred_element_type=F32)
        if first:
            vacc[...] = term
        else:
            vacc[...] += term

    def grad_term(t, xx):
        dsh[t, xx] = jnp.dot(wg[t, xx], gvr[...], preferred_element_type=F32).astype(BF16)

    def dc_copy(t, xx):
        return remote(dsh.at[t, xx], dex.at[xx], s_dc.at[xx], r_dc.at[xx], dev(c=1 - c))

    def dy_copy(yy):
        return remote(dsum.at[yy], dy.at[y], s_dy.at[yy], r_dy.at[y], dev(y=yy))

    def share(t):
        @pl.when(a != t)
        def _():
            def step(xx, carry):
                dc_copy(t, xx).start()
                return carry
            lax.fori_loop(0, XN, step, 0)

        @pl.when(a == t)
        def _():
            def step(o, carry):
                xx = (y + o) % YN
                dc_copy(t, xx).wait_recv()
                dsum[xx] = (dsh[t, xx].astype(F32) + dex[xx].astype(F32)).astype(BF16)

                @pl.when(o > 0)
                def _():
                    dy_copy(xx).start()
                return carry
            lax.fori_loop(0, YN, step, 0)

    for o in ORDER:
        if o:
            w_wait(o)
        value_term(0, (x + o) % XN, o == 0)
    arrive(A_GV, lambda g: gvr.at[rows32(g)], gvs.at[0])

    def grad_step0(xx, carry):
        grad_term(0, xx)
        return carry

    lax.fori_loop(0, XN, grad_step0, 0)
    share(0)

    for o in ORDER:
        if o:
            w1_wait(o)
        value_term(1, (x + o) % XN, False)
    vt[...] = jnp.transpose(vacc[...]).astype(BF16)
    slot = x * 2 + pair

    def own_v():
        vr[h, slot] = vt[rows32(i), :]

    spread(A_V, lambda g: vt.at[rows32(g)], vr.at[h, slot], own_v)

    def grad_step1(xx, carry):
        grad_term(1, xx)
        return carry

    lax.fori_loop(0, XN, grad_step1, 0)
    share(1)

    arrive(A_V, lambda g: vr.at[g % 2, g // 2], vt.at[rows32(0)])

    def load_v(p, c0, l0):
        at = (pl.ds(c0, 16), pl.ds((p % 2) * ROWS + l0, 128))
        return vr[0, p // 2, at[0], at[1]].astype(F32) + vr[1, p // 2, at[0], at[1]].astype(F32)

    to_spectrum(load_v, spec)

    def store_c(p, c0, l0, v):
        cs[p, pl.ds(c0, 16), pl.ds(l0, 128)] = v

    from_spectrum(1, store_c)

    def own_c():
        cr[rows32(i), :] = cs[i]

    spread(A_C, lambda g: cs.at[g], cr.at[rows32(i)], own_c)

    for o in ORDER[1:]:
        yy = (y + o) % YN
        remote(dsum.at[yy], dy.at[yy], s_dy.at[yy], r_dy.at[yy], dev(c=1 - c)).wait_recv()
    dy[y] = dsum[y]

    def dz_copy(hr):
        return remote(tz.at[hr], dz.at[zl], s_dz.at[hr], r_dz.at[zl], dev(zh=2 * pair + hr, zl=zl_s))

    for hr in (0, 1):
        cols = slice(hr * ROWS, (hr + 1) * ROWS)
        total = dy[0, :, cols].astype(F32) + dy[1, :, cols].astype(F32) + dy[2, :, cols].astype(F32) + dy[3, :, cols].astype(F32)
        tz[hr] = total.astype(BF16)
        stays = jnp.logical_and(hr == h, zl_s == zl)

        @pl.when(jnp.logical_not(stays))
        def _(hr=hr):
            dz_copy(hr).start()

        @pl.when(stays)
        def _(hr=hr):
            dz[zl] = tz[hr]

    for zz in (0, 1):
        @pl.when(jnp.logical_not(jnp.logical_and(zz == zl, here)))
        def _(zz=zz):
            remote(tz.at[0], dz.at[zz], s_dz.at[0], r_dz.at[zz], dev(c=1 - c)).wait_recv()

    gt_ref[...] = jnp.transpose(dz[0].astype(F32) + dz[1].astype(F32)).astype(BF16)

    arrive(A_C, lambda g: cr.at[rows32(g)], cs.at[0])
    conv = jnp.transpose(cr[...].astype(F32))
    out_ref[...] = (gate_ref[...].astype(F32) * conv).astype(BF16)
    gg_ref[...] = (cot_ref[...].astype(F32) * conv).astype(BF16)

    sent(A_F, ft.at[rows32(0)])
    sent(A_G, gt.at[rows32(0)])
    sent(A_GV, gvs.at[0])
    sent(A_V, vt.at[rows32(0)])
    sent(A_C, cs.at[0])
    xz_copy(1).wait_send()

    @pl.when(jnp.logical_not(here))
    def _():
        xz_copy(0).wait_send()

    for o in ORDER[1:]:
        w_copy(o).wait_send()
        xy_copy(o).wait_send()
        dy_copy((y + o) % YN).wait_send()
        for k in range(EXCH):
            w1_copy(k, o).wait_send()
    for k in range(EXCH):
        e_copy(k).wait_send()
    for q in range(4):
        xc_copy(q).wait_send()
        dc_copy(1 - a, q).wait_send()
    for hr in (0, 1):
        @pl.when(jnp.logical_not(jnp.logical_and(hr == h, zl_s == zl)))
        def _(hr=hr):
            dz_copy(hr).wait_send()


def per_device(tokens, in_weight, filters, gate, cotangent):
    forward, inverse, twist = _tables()
    vm = pltpu.VMEM
    dma = pltpu.SemaphoreType.DMA
    scratch = [
        vm((2, XN, WIDE, WIDE), BF16),
        vm((2, YN, WIDE, WIDE), BF16),
        vm((WIDE, ROWS), BF16),
        vm((WIDE, ROWS), BF16),
        vm((GROUP, CH, ROWS), BF16),
        vm((GROUP, CH, ROWS), BF16),
        vm((WIDE, WIDE), BF16),
        vm((2, GROUP // 2, CH, WIDE), BF16),
        vm((GROUP // 2, CH, WIDE), BF16),
        vm((WIDE, WIDE), BF16),
        vm((GROUP, CH, ROWS), BF16),
        vm((WIDE, ROWS), BF16),
        vm((ZROWS, WIDE), BF16),
        vm((ZROWS, WIDE), BF16),
        vm((ZROWS, WIDE), F32),
        vm((ZROWS, WIDE), F32),
        vm((WIDE, WIDE), F32),
        vm((2, XN, WIDE, WIDE), BF16),
        vm((XN, WIDE, WIDE), BF16),
        vm((YN, WIDE, WIDE), BF16),
        vm((YN, WIDE, WIDE), BF16),
        vm((2, WIDE, ROWS), BF16),
        vm((2, WIDE, ROWS), BF16),
        dma((5, GROUP)), dma((5, GROUP)),
        dma((4,)), dma((4,)),
        dma((EXCH,)), dma((EXCH,)),
        dma((EXCH, 4)), dma((EXCH, 4)),
        dma((2,)), dma((2,)),
        dma((4,)), dma((4,)),
        dma((4,)), dma((4,)),
        dma((4,)), dma((4,)),
        dma((4,)), dma((4,)),
        dma((2,)), dma((2,)),
        dma((1,)),
    ]
    block = jax.ShapeDtypeStruct((ROWS, WIDE), BF16)
    return pl.pallas_call(
        _kernel,
        out_shape=(block, block, block),
        in_specs=[pl.BlockSpec(memory_space=pltpu.VMEM)] * 8,
        out_specs=[pl.BlockSpec(memory_space=pltpu.VMEM)] * 3,
        scratch_shapes=scratch,
        compiler_params=pltpu.CompilerParams(
            collective_id=0, has_side_effects=True, vmem_limit_bytes=56 * 2**20),
        name="hyena",
    )(tokens, in_weight, filters, gate, cotangent, jnp.asarray(forward), jnp.asarray(inverse), jnp.asarray(twist))


def solution(mesh):
    placed = (P("ctx", "tp"),) * 5
    return jax.shard_map(per_device, mesh=mesh, in_specs=placed, out_specs=(P("ctx", "tp"),) * 3, check_vma=False)
```

time: 374 us -> 122 us (0.33); the launches traced: 370 us -> 122 us
  waiting for transfers between devices: 250 us -> 0 us
  Pallas kernels: 0 us -> 118 us
  matrix products: 58.4 us -> 0 us
  blocking collectives: 22.3 us -> 0 us
  between operations: 14.2 us -> 0.65 us
  starting transfers between devices: 12.3 us -> 0 us
  local copies, waits for them, and re-layouts: 8.2 us -> 3.46 us
  other arithmetic: 3.94 us -> 0 us
    all_gather x2 -> x0, waiting for transfers between devices: 157 us -> none  [the longest x1 113 us: per_device(): weight_all = lax.all_gather(in_weight, 'ctx', axis=0, tiled=True)]
    pallas_call x0 -> x1, Pallas kernels: none -> 118 us  [per_device(): pl.pallas_call(_kernel, out_shape=(block, block, block), in_specs=[pl.Blo...]
    reduce_scatter x1 -> x0, waiting for transfers between devices: 65 us -> none  [per_device(): lax.psum_scatter(partial_value.astype(jnp.bfloat16), 'tp', scatter_dimens...]
    dot_general x14 -> x0, matrix products: 58.4 us -> none  [the longest x1 7.76 us: per_device(): lax.dot_general(grad_values, weight_all, (((1,), (1,)), ((), ())), prefer...]
    all_to_all x1 -> x0, waiting for transfers between devices: 26.7 us -> none  [per_device(): lax.all_to_all(jnp.stack([filters, signals, grad_conv]).astype(jnp.bfloat...]
    all_to_all x1 -> x0, blocking collectives: 22.3 us -> none  [per_device(): lax.all_to_all(shortened(result), 'ctx', split_axis=1, concat_axis=2, til...]
    all_to_all x1 -> x0, starting transfers between devices: 12 us -> none  [per_device(): lax.all_to_all(jnp.stack([filters, signals, grad_conv]).astype(jnp.bfloat...]
  transfers between devices with their start and end apart: 4 -> 0, of which waited for: 4 -> 0; matrix products, arithmetic and copies ran while one was open for 1% -> 0% of each run, Pallas kernels for 0% -> 0%
where the time goes in v1:
time: 122 us
  Pallas kernels  118 us (97%)
  local copies, waits for them, and re-layouts  3.46 us (3%)
    pallas_call x1, Pallas kernels, per_device(): pl.pallas_call(_kernel, out_shape=(block, block, block), in_specs=[pl.Blo...  118 us
    unnamed x7, local copies, waits for them, and re-layouts  3.46 us

profile of v1, /device:TPU:1, one launch (start us, length us, event | category | flops | bytes accessed | tf_op | source)
XLA Modules:
  0.0 121.7 jit_solution(10142401842789420679)
XLA Ops:
  0.6 117.6 %hyena.1 = (bf16[256,512]{1,0:T(8,128)(2,1)}, bf16[256,512]{1,0:T(8,128)(2,1)}, bf16[256,512]{1,0:T(8,128)(2,1)}) custom-call(bf16[256,512]{1,0:T(8,128)(2,1)} %x_ref.1, bf16[512,512]{1,0:T(8,128)(2,1)} %w_ref.1, f32[256,512]{1,0:T(8,128)} %f_ref.1, bf16[256,512]{1,0:T(8,128)(2,1)} %gate_ref.1, bf16[256,512]{1,0:T(8,128)(2,1)} %cot_ref.1, ...), custom_call_target="tpu_custom_call" | custom-call | tf_op jit(solution)/shard_map/hyena/pallas_call | solution.py:533
  118.2 0.0 copy-start.1
  118.2 1.7 %copy.14 = bf16[256,512]{1,0:T(8,128)(2,1)} copy(bf16[256,512]{1,0:T(8,128)(2,1)} %get-tuple-element.6) | data formatting | bytes 524288
  119.9 0.0 copy-done.1
  119.9 0.0 copy-start
  119.9 0.7 copy.15
  120.6 0.3 copy-done
  121.0 0.7 copy.16
Async XLA Ops:
  118.2 1.7 %copy-start.1 = (bf16[256,512]{1,0:T(8,128)(2,1)S(1)}, bf16[256,512]{1,0:T(8,128)(2,1)}, u32[]{:S(2)}) copy-start(bf16[256,512]{1,0:T(8,128)(2,1)} %get-tuple-element.7) | copy-start | bytes 786436
  119.9 1.0 copy-start

commit v2 on v1

v2 whole, which is shorter than its diff:
```python
import functools
import math

import jax
import jax.numpy as jnp
import numpy as np
from jax import lax
from jax.experimental import pallas as pl
from jax.experimental.pallas import tpu as pltpu
from jax.sharding import PartitionSpec as P

MESH = pl.DeviceIdType.MESH
F32 = jnp.float32
BF16 = jnp.bfloat16
TWO_PI = 2.0 * math.pi

XN, HN, YN = 4, 4, 4
GROUP = XN * HN
ROWS = 256
WIDE = 512
CH = WIDE // GROUP
HALF = GROUP + 1
PART = CH // 2
ZROWS = HALF * PART
HW = WIDE // 2
ORDER = (0, 1, 3, 2)

A_FG, A_GV, A_V, A_C = range(4)


def _add(a, b):
    if a is None:
        return b
    return a if b is None else a + b


def _sub(a, b):
    if b is None:
        return a
    return -b if a is None else a - b


def _turn(value, angle):
    re, im = value
    if re is None and im is None:
        return value
    quarter = angle / (math.pi / 2)
    if abs(quarter - round(quarter)) < 1e-9:
        q = round(quarter) % 4
        neg = lambda v: None if v is None else -v
        return [(re, im), (neg(im), re), (neg(re), neg(im)), (im, neg(re))][q]
    c, s = float(math.cos(angle)), float(math.sin(angle))
    mul = lambda v, f: None if v is None else v * f
    return _sub(mul(re, c), mul(im, s)), _add(mul(re, s), mul(im, c))


def _dft(values, sign):
    n = len(values)
    if n == 1:
        return values
    even, odd = _dft(values[0::2], sign), _dft(values[1::2], sign)
    out = [None] * n
    for k in range(n // 2):
        t = _turn(odd[k], sign * TWO_PI * k / n)
        out[k] = (_add(even[k][0], t[0]), _add(even[k][1], t[1]))
        out[k + n // 2] = (_sub(even[k][0], t[0]), _sub(even[k][1], t[1]))
    return out


def _pieces_forward(xs):
    even = _dft([(v, None) for v in xs], -1)
    odd = _dft([_turn((v, None), -TWO_PI * p / 32) for p, v in enumerate(xs)], -1)
    out = []
    for k in range(HALF):
        out.append(even[k // 2] if k % 2 == 0 else odd[k // 2])
    return out


def _pieces_inverse(zs):
    first = [(zs[0][0] * 0.5, None)] + [zs[2 * m] for m in range(1, 8)] + [(None, None)] * 8
    second = [zs[2 * m + 1] for m in range(8)] + [(None, None)] * 8
    even, odd = _dft(first, 1), _dft(second, 1)
    last = zs[16][0] * 0.5
    out = []
    for p in range(GROUP):
        turned = _turn(odd[p], TWO_PI * p / 32)[0]
        total = _add(even[p][0], turned)
        out.append(total + last if p % 2 == 0 else total - last)
    return out


def _tables():
    s = np.arange(ROWS, dtype=np.int64)
    angle = (s[:, None] * s[None, :] % ROWS) * (TWO_PI / ROWS)
    cos, sin = np.cos(angle), np.sin(angle)
    forward = np.block([[cos, -sin], [sin, cos]])
    k = np.arange(HALF)
    turn = (k[:, None] * s[None, :]) * (TWO_PI / 8192)
    twist = np.concatenate([np.cos(turn), np.sin(turn)], axis=1)
    twist = np.concatenate([twist, np.zeros((24 - HALF, 2 * ROWS))], axis=0)
    return forward.astype(np.float32), twist.astype(np.float32)


def _kernel(x_hbm, w_hbm, f_hbm, gate_hbm, cot_hbm, dft_hbm, tw_hbm,
            conv_ref, g0_ref, g1_ref,
            x_ref, f_ref, gate_ref, cot_ref, dft_ref, tw_ref, fwd_ref, inv_ref,
            wg, xg, fg, fgr, vt, vr, gvs, gvr, cs, cr,
            zhi, zlo, spec_f, spec, vacc, dsh, dex, dsum, dy, tz, dz,
            s_a2a, r_a2a, s_gv, s_w, r_w, s_e, r_e, s_xz, r_xz, s_xy, r_xy, s_xc, r_xc,
            s_dc, r_dc, s_dy, r_dy, s_dz, r_dz, l_in):
    i = lax.axis_index("ctx")
    j = lax.axis_index("tp")
    x, zh = i // HN, i % HN
    pair, h = zh // 2, zh % 2
    y, zl, c = j // 4, (j // 2) % 2, j % 2
    a = (c + h) % 2
    pending = []

    def dev(x=x, zh=zh, y=y, zl=zl, c=c):
        return (x * HN + zh, y * 4 + zl * 2 + c)

    other = dev(c=1 - c)

    def remote(src, dst, ssem, rsem, target):
        return pltpu.make_async_remote_copy(
            src_ref=src, dst_ref=dst, send_sem=ssem, recv_sem=rsem, device_id=target, device_id_type=MESH)

    def send(copy):
        copy.start()
        pending.append(copy.wait_send)

    def send_if(cond, copy):
        pl.when(cond)(copy.start)
        pending.append(lambda: pl.when(cond)(copy.wait_send))

    loads = [pltpu.make_async_copy(src, dst, l_in.at[n]) for n, (src, dst) in enumerate((
        (f_hbm, f_ref), (gate_hbm, gate_ref), (cot_hbm, cot_ref), (x_hbm, x_ref), (w_hbm, wg.at[0, x]),
        (tw_hbm, tw_ref), (dft_hbm, dft_ref)))]
    for load in loads:
        load.start()

    barrier = pltpu.get_barrier_semaphore()

    def greet(target):
        pl.semaphore_signal(barrier, inc=1, device_id=target, device_id_type=MESH)

    def greet_ctx(o, carry):
        greet(((i + o) % GROUP, j))
        return carry

    lax.fori_loop(1, GROUP, greet_ctx, 0)
    for o in (1, 2, 3):
        greet(dev(y=(y + o) % YN))
    greet(other)
    greet(dev(zh=2 * pair, zl=1 - zl))
    greet(dev(zh=2 * pair + 1, zl=1 - zl))

    loads[0].wait()
    fg[:, :ROWS] = jnp.transpose(f_ref[...]).astype(BF16)
    loads[1].wait()
    loads[2].wait()
    fg[:, ROWS:] = jnp.transpose(cot_ref[...].astype(F32) * gate_ref[...].astype(F32)).astype(BF16)
    for load in loads[3:]:
        load.wait()
    hi = dft_ref[...].astype(BF16)
    fwd_ref[0] = hi
    fwd_ref[1] = (dft_ref[...] - hi.astype(F32)).astype(BF16)
    low, high = slice(0, ROWS), slice(ROWS, WIDE)
    for n in (0, 1):
        for rows, cols in ((low, low), (low, high), (high, low), (high, high)):
            inv_ref[n, rows, cols] = fwd_ref[n, cols, rows] * (1.0 / 4096.0)
    pl.semaphore_wait(barrier, GROUP - 1 + 3 + 1 + 2)

    def spread(kind, k, src_of, dst, own):
        def copy(o):
            g = (i + o) % GROUP
            return remote(src_of(g), dst, s_a2a.at[kind, k, g], r_a2a.at[kind, k, i], (g, j))

        def start(o, carry):
            copy(o).start()
            return carry

        def finish(o, carry):
            copy(o).wait_send()
            return carry

        lax.fori_loop(1, GROUP, start, 0)
        own()
        pending.append(lambda: lax.fori_loop(1, GROUP, finish, 0))

    def arrive(kind, k, dst_of, src):
        def step(o, carry):
            g = (i + o) % GROUP
            remote(src, dst_of(g), s_a2a.at[kind, k, g], r_a2a.at[kind, k, g], (g, j)).wait_recv()
            return carry
        lax.fori_loop(1, GROUP, step, 0)

    def chans(k, g):
        return pl.ds(pl.multiple_of(k * HW + g * PART, PART), PART)

    zh_d = 2 * pair + (c + zl + pair) % 2
    t_d = (zl + pair) % 2
    zl_s = (c + h + pair) % 2
    myrows = pl.ds(pl.multiple_of(h * ROWS, ROWS), ROWS)
    here = zh_d == zh
    stays = [jnp.logical_and(hr == h, zl_s == zl) for hr in (0, 1)]

    def xz_copy(which):
        target = dev(zh=zh_d, zl=zl if which == 0 else 1 - zl)
        return remote(x_ref, xg.at[t_d, y, myrows], s_xz.at[which], r_xz.at[h], target)

    def tokens_along_z():
        send(xz_copy(1))
        send_if(jnp.logical_not(here), xz_copy(0))

        @pl.when(here)
        def _():
            xg[t_d, y, myrows] = x_ref[...]

    def send_fg(k):
        def own():
            fgr[k, i] = fg[chans(k, i), :]

        spread(A_FG, k, lambda g: fg.at[chans(k, g)], fgr.at[k, i], own)

    right, left = dev(x=(x + 1) % XN), dev(x=(x + XN - 1) % XN)

    def block_of(o):
        return (x + o) % XN

    def piece(k, r):
        return (pl.ds(r * HW, HW), pl.ds(k * HW, HW) if k < 2 else slice(None))

    def ring(t, k, r, o, n, target):
        at = (t, block_of(o)) + piece(k, r)
        return remote(wg.at[at], wg.at[at], s_w.at[k, r, n], r_w.at[k, r, block_of(o)], target)

    def ring_wait(t, k, r, o):
        ring(t, k, r, o, 0, other).wait_recv()

    def ring_start(t, k, r):
        send(ring(t, k, r, 0, 0, right))
        send(ring(t, k, r, 0, 1, left))

    def ring_forward(t, k):
        ring_wait(t, k, 0, 3)
        send(ring(t, k, 0, 3, 2, right))
        ring_wait(t, k, 1, 1)
        send(ring(t, k, 1, 1, 2, left))

    def ring_arrive(t, k, o):
        if o in (1, 2):
            ring_wait(t, k, 0, o)
        if o in (2, 3):
            ring_wait(t, k, 1, o)

    def e_copy(k, r):
        return remote(wg.at[(0, x) + piece(k, r)], wg.at[(1, x) + piece(k, r)],
                      s_e.at[k, r], r_e.at[k, r], dev(zh=3 - zh))

    def exchange_arrive(k):
        for r in (0, 1):
            e_copy(k, r).wait_recv()
            ring_start(1, k, r)

    def to_spectrum(load, out):
        def step(it, carry):
            l0 = pl.multiple_of(it * 128, 128)
            zs = _pieces_forward([load(p, l0) for p in range(GROUP)])
            for k in range(HALF):
                re, im = zs[k]
                if k > 0:
                    co = tw_ref[k:k + 1, pl.ds(l0, 128)]
                    si = tw_ref[k:k + 1, pl.ds(l0 + ROWS, 128)]
                    if im is None:
                        re, im = re * co, -(re * si)
                    else:
                        re, im = re * co + im * si, im * co - re * si
                if im is None:
                    im = jnp.zeros_like(re)
                at = slice(k * PART, (k + 1) * PART)
                for part, off in ((re, 0), (im, ROWS)):
                    hi = part.astype(BF16)
                    zhi[at, pl.ds(l0 + off, 128)] = hi
                    zlo[at, pl.ds(l0 + off, 128)] = (part - hi.astype(F32)).astype(BF16)
            return carry
        lax.fori_loop(0, 2, step, 0)
        out[...] = (jnp.dot(zhi[...], fwd_ref[0], preferred_element_type=F32)
                    + jnp.dot(zlo[...], fwd_ref[0], preferred_element_type=F32)
                    + jnp.dot(zhi[...], fwd_ref[1], preferred_element_type=F32))

    def from_spectrum(sign, filt, store):
        def product(n, carry):
            at = pl.ds(pl.multiple_of(n * PART, PART), PART)
            ar, ai = spec[at, :ROWS], spec[at, ROWS:]
            br, bi = filt[at, :ROWS], filt[at, ROWS:]
            if sign > 0:
                re, im = ar * br - ai * bi, ar * bi + ai * br
            else:
                re, im = ar * br + ai * bi, ai * br - ar * bi
            for part, cols in ((re, slice(0, ROWS)), (im, slice(ROWS, 2 * ROWS))):
                hi = part.astype(BF16)
                zhi[at, cols] = hi
                zlo[at, cols] = (part - hi.astype(F32)).astype(BF16)
            return carry
        lax.fori_loop(0, HALF, product, 0)
        spec[...] = (jnp.dot(zhi[...], inv_ref[0], preferred_element_type=F32)
                     + jnp.dot(zlo[...], inv_ref[0], preferred_element_type=F32)
                     + jnp.dot(zhi[...], inv_ref[1], preferred_element_type=F32))

        def step(it, carry):
            l0 = pl.multiple_of(it * 128, 128)
            zs = []
            for k in range(HALF):
                at = slice(k * PART, (k + 1) * PART)
                re, im = spec[at, pl.ds(l0, 128)], spec[at, pl.ds(l0 + ROWS, 128)]
                if k > 0:
                    co = tw_ref[k:k + 1, pl.ds(l0, 128)]
                    si = tw_ref[k:k + 1, pl.ds(l0 + ROWS, 128)]
                    re, im = re * co - im * si, im * co + re * si
                zs.append((re, im))
            for p, v in enumerate(_pieces_inverse(zs)):
                store(p, l0, v.astype(BF16))
            return carry
        lax.fori_loop(0, 2, step, 0)

    up, down = dev(y=(y + 1) % YN), dev(y=(y + YN - 1) % YN)

    def xy_copy(o, hr, n, target):
        at = (a, (y + o) % YN, pl.ds(hr * ROWS, ROWS))
        return remote(xg.at[at], xg.at[at], s_xy.at[hr, n], r_xy.at[hr, (y + o) % YN], target)

    def xc_copy(yy, hr):
        at = (a, yy, pl.ds(hr * ROWS, ROWS))
        return remote(xg.at[at], xg.at[at], s_xc.at[hr, yy], r_xc.at[hr, yy], other)

    def tokens_along_y():
        for hr in (0, 1):
            wait = remote(x_ref, xg.at[a, y, pl.ds(hr * ROWS, ROWS)], s_xz.at[0], r_xz.at[hr], other).wait_recv
            pl.when(jnp.logical_not(stays[hr]))(wait)
            send(xy_copy(0, hr, 0, up))
            send(xy_copy(0, hr, 1, down))
            send(xc_copy(y, hr))

    def tokens_arrive(o, hr):
        xy_copy(o, hr, 0, other).wait_recv()
        if (o, hr) == (3, 0):
            send(xy_copy(o, hr, 2, up))
        if (o, hr) == (1, 1):
            send(xy_copy(o, hr, 2, down))
        send(xc_copy((y + o) % YN, hr))

    def tokens_from_core():
        for yy in range(YN):
            for hr in (0, 1):
                at = (1 - a, yy, pl.ds(hr * ROWS, ROWS))
                remote(xg.at[at], xg.at[at], s_xc.at[hr, yy], r_xc.at[hr, yy], other).wait_recv()

    def fg_arrive(k):
        arrive(A_FG, k, lambda g: fgr.at[k, g], fg.at[chans(k, 0)])

    def conv_grad(k):
        to_spectrum(lambda p, l0: fgr[k, p, :, pl.ds(l0, 128)].astype(F32), spec_f.at[k])
        to_spectrum(lambda p, l0: fgr[k, p, :, pl.ds(ROWS + l0, 128)].astype(F32), spec)

        def store(p, l0, v):
            gvs[k, p // 2, :, pl.ds((p % 2) * ROWS + l0, 128)] = v

        from_spectrum(-1, spec_f.at[k], store)

        for zt in (zh, 3 - zh):
            for o in range(XN):
                g = block_of(o) * HN + zt
                if o == 0 and zt is zh:
                    gvr[chans(k, i), :] = gvs[k, i // 2]
                else:
                    send(remote(gvs.at[k, g // 2], gvr.at[chans(k, i)], s_a2a.at[A_GV, k, g], r_a2a.at[A_GV, k, i], (g, j)))

    partner = 2 * pair + 1 - h

    def gv_pass(k):
        for zt in (zh, 3 - zh):
            for o in range(XN):
                g = block_of(o) * HN + zt
                at = gvr.at[chans(k, g)]
                if not (o == 0 and zt is zh):
                    remote(at, at, s_gv.at[k, g], r_a2a.at[A_GV, k, g], other).wait_recv()
                send(remote(at, at, s_gv.at[k, g], r_a2a.at[A_GV, k, g], dev(zh=partner)))

    def gv_arrive(k):
        for zt in (partner, 3 - partner):
            for o in range(XN):
                g = block_of(o) * HN + zt
                at = gvr.at[chans(k, g)]
                remote(at, at, s_gv.at[k, g], r_a2a.at[A_GV, k, g], other).wait_recv()

    def value_term(k, t, xx, first):
        term = jnp.dot(xg[t, xx], wg[t, xx, :, k * HW:(k + 1) * HW], preferred_element_type=F32)
        if first:
            vacc[k] = term
        else:
            vacc[k] += term

    def send_values(k):
        vt[k * HW:(k + 1) * HW, :] = jnp.transpose(vacc[k]).astype(BF16)
        slot = x * 2 + pair

        def own():
            vr[k, h, slot] = vt[chans(k, i), :]

        spread(A_V, k, lambda g: vt.at[chans(k, g)], vr.at[k, h, slot], own)

    def conv_forward(k):
        arrive(A_V, k, lambda g: vr.at[k, g % 2, g // 2], vt.at[chans(k, 0)])

        def load(p, l0):
            cols = pl.ds((p % 2) * ROWS + l0, 128)
            return vr[k, 0, p // 2, :, cols].astype(F32) + vr[k, 1, p // 2, :, cols].astype(F32)

        to_spectrum(load, spec)

        def store(p, l0, v):
            cs[k, p, :, pl.ds(l0, 128)] = v

        from_spectrum(1, spec_f.at[k], store)

        def own():
            cr[chans(k, i), :] = cs[k, i]

        spread(A_C, k, lambda g: cs.at[k, g], cr.at[chans(k, i)], own)

    def grad_term(t, xx):
        dsh[t, xx] = jnp.dot(wg[t, xx], gvr[...], preferred_element_type=F32).astype(BF16)

    def dc_copy(t, xx):
        return remote(dsh.at[t, xx], dex.at[xx], s_dc.at[xx], r_dc.at[xx], other)

    def dy_copy(yy, hr):
        return remote(dsum.at[yy, hr], dy.at[y, hr], s_dy.at[hr, yy], r_dy.at[hr, y], dev(y=yy))

    def grad_block(t, o):
        xx = block_of(o)
        grad_term(t, xx)
        pl.when(a != t)(dc_copy(t, xx).start)

    def grad_sum(t, o):
        xx = block_of(o)

        @pl.when(a == t)
        def _():
            dc_copy(t, xx).wait_recv()
            for hr in (0, 1):
                cols = slice(hr * ROWS, (hr + 1) * ROWS)
                dsum[xx, hr] = (dsh[t, xx, :, cols].astype(F32) + dex[xx, :, cols].astype(F32)).astype(BF16)
                pl.when(xx != y)(dy_copy(xx, hr).start)

    def dz_copy(hr):
        return remote(tz.at[hr], dz.at[zl], s_dz.at[hr], r_dz.at[zl], dev(zh=2 * pair + hr, zl=zl_s))

    def grad_along_z(hr):
        total = dsum[y, hr].astype(F32)
        for o in ORDER[1:]:
            yy = (y + o) % YN
            remote(dsum.at[yy, hr], dy.at[yy, hr], s_dy.at[hr, yy], r_dy.at[hr, yy], other).wait_recv()
        for o in ORDER[1:]:
            total += dy[(y + o) % YN, hr].astype(F32)
        tz[hr] = total.astype(BF16)
        send_if(jnp.logical_not(stays[hr]), dz_copy(hr))

        @pl.when(stays[hr])
        def _():
            dz[zl] = tz[hr]

    def grad_done():
        for zz in (0, 1):
            wait = remote(tz.at[0], dz.at[zz], s_dz.at[0], r_dz.at[zz], other).wait_recv
            pl.when(jnp.logical_not(jnp.logical_and(zz == zl, here)))(wait)
        g0_ref[...] = jnp.transpose(dz[0].astype(F32)).astype(BF16)
        g1_ref[...] = jnp.transpose(dz[1].astype(F32)).astype(BF16)

    def exchange(k):
        for r in (0, 1):
            send(e_copy(k, r))

    send_fg(0)
    send_fg(1)
    for r in (0, 1):
        ring_start(0, 2, r)
    fg_arrive(0)
    tokens_along_z()
    fg_arrive(1)
    exchange(0)
    conv_grad(0)
    ring_forward(0, 2)
    conv_grad(1)
    tokens_along_y()
    exchange_arrive(0)
    exchange(1)
    gv_pass(0)
    tokens_arrive(3, 0)
    tokens_arrive(1, 1)
    gv_pass(1)
    ring_forward(1, 0)
    exchange_arrive(1)
    tokens_arrive(1, 0)
    tokens_arrive(3, 1)
    for k in (0, 1):
        gv_arrive(k)
    for n, o in enumerate(ORDER):
        ring_arrive(0, 2, o)
        grad_block(0, o)
        if n:
            grad_sum(0, ORDER[n - 1])
    grad_sum(0, ORDER[3])
    tokens_arrive(2, 0)
    tokens_arrive(2, 1)
    ring_forward(1, 1)
    tokens_from_core()
    for o in ORDER:
        value_term(0, 0, block_of(o), o == 0)
    for o in ORDER:
        ring_arrive(1, 0, o)
        value_term(0, 1, block_of(o), False)
    send_values(0)
    for o in ORDER:
        value_term(1, 0, block_of(o), o == 0)
    for n, o in enumerate(ORDER):
        ring_arrive(1, 1, o)
        value_term(1, 1, block_of(o), False)
        if n == 3:
            send_values(1)
        grad_block(1, o)
        if n:
            grad_sum(1, ORDER[n - 1])
    grad_sum(1, ORDER[3])
    conv_forward(0)
    grad_along_z(0)
    grad_along_z(1)
    conv_forward(1)
    for k in (0, 1):
        arrive(A_C, k, lambda g: cr.at[chans(k, g)], cs.at[k, 0])
    conv_ref[...] = jnp.transpose(cr[...].astype(F32)).astype(BF16)
    grad_done()

    for wait in pending:
        wait()
    for q in range(4):
        dc_copy(1 - a, q).wait_send()
    for o in ORDER[1:]:
        for hr in (0, 1):
            dy_copy((y + o) % YN, hr).wait_send()


def per_device(tokens, in_weight, filters, gate, cotangent):
    forward, twist = _tables()
    vm = pltpu.VMEM
    dma = pltpu.SemaphoreType.DMA
    scratch = [
        vm((ROWS, WIDE), BF16),
        vm((ROWS, WIDE), F32),
        vm((ROWS, WIDE), BF16),
        vm((ROWS, WIDE), BF16),
        vm((WIDE, WIDE), F32),
        vm((24, WIDE), F32),
        vm((2, WIDE, WIDE), BF16),
        vm((2, WIDE, WIDE), BF16),
        vm((2, XN, WIDE, WIDE), BF16),
        vm((2, YN, WIDE, WIDE), BF16),
        vm((WIDE, 2 * ROWS), BF16),
        vm((2, GROUP, PART, 2 * ROWS), BF16),
        vm((WIDE, WIDE), BF16),
        vm((2, 2, GROUP // 2, PART, WIDE), BF16),
        vm((2, GROUP // 2, PART, WIDE), BF16),
        vm((WIDE, WIDE), BF16),
        vm((2, GROUP, PART, ROWS), BF16),
        vm((WIDE, ROWS), BF16),
        vm((ZROWS, WIDE), BF16),
        vm((ZROWS, WIDE), BF16),
        vm((2, ZROWS, WIDE), F32),
        vm((ZROWS, WIDE), F32),
        vm((2, WIDE, HW), F32),
        vm((2, XN, WIDE, WIDE), BF16),
        vm((XN, WIDE, WIDE), BF16),
        vm((YN, 2, WIDE, ROWS), BF16),
        vm((YN, 2, WIDE, ROWS), BF16),
        vm((2, WIDE, ROWS), BF16),
        vm((2, WIDE, ROWS), BF16),
        dma((4, 2, GROUP)), dma((4, 2, GROUP)),
        dma((2, GROUP)),
        dma((3, 2, 3)), dma((3, 2, 4)),
        dma((2, 2)), dma((2, 2)),
        dma((2,)), dma((2,)),
        dma((2, 3)), dma((2, 4)),
        dma((2, 4)), dma((2, 4)),
        dma((4,)), dma((4,)),
        dma((2, 4)), dma((2, 4)),
        dma((2,)), dma((2,)),
        dma((7,)),
    ]
    block = jax.ShapeDtypeStruct((ROWS, WIDE), BF16)
    conv, g0, g1 = pl.pallas_call(
        _kernel,
        out_shape=(block, block, block),
        in_specs=[pl.BlockSpec(memory_space=pl.ANY)] * 7,
        out_specs=[pl.BlockSpec(memory_space=pltpu.VMEM)] * 3,
        scratch_shapes=scratch,
        compiler_params=pltpu.CompilerParams(
            collective_id=0, has_side_effects=True, vmem_limit_bytes=56 * 2**20),
        name="hyena",
    )(tokens, in_weight, filters, gate, cotangent, jnp.asarray(forward), jnp.asarray(twist))
    conv = conv.astype(F32)
    gated_output = (gate.astype(F32) * conv).astype(BF16)
    grad_gate = (cotangent.astype(F32) * conv).astype(BF16)
    grad_tokens = (g0.astype(F32) + g1.astype(F32)).astype(BF16)
    return gated_output, grad_gate, grad_tokens


def solution(mesh):
    placed = (P("ctx", "tp"),) * 5
    return jax.shard_map(per_device, mesh=mesh, in_specs=placed, out_specs=(P("ctx", "tp"),) * 3, check_vma=False)
```

time: 122 us -> 106 us (0.87)
  the two profiles are of different devices: /device:TPU:1 before, /device:TPU:192 now
where the time goes in v2:
time: 106 us
  Pallas kernels  103 us (97%)
  other arithmetic  2.14 us (2%)
    pallas_call x1, Pallas kernels, per_device(): pl.pallas_call(_kernel, out_shape=(block, block, block), in_specs=[pl.Blo...  103 us
    convert_element_type x1, other arithmetic, per_device(): grad_gate = (cotangent.astype(F32) * conv).astype(BF16)  2.14 us

profile of v2, /device:TPU:192, one launch (start us, length us, event | category | flops | bytes accessed | tf_op | source)
XLA Modules:
  0.0 105.7 jit_solution(5492359744571728715)
XLA Ops:
  0.6 0.0 copy-start.1
  0.6 0.0 copy-start
  0.7 102.9 %hyena.1 = (bf16[256,512]{1,0:T(8,128)(2,1)}, bf16[256,512]{1,0:T(8,128)(2,1)}, bf16[256,512]{1,0:T(8,128)(2,1)}) custom-call(bf16[256,512]{1,0:T(8,128)(2,1)} %x_hbm.1, bf16[512,512]{1,0:T(8,128)(2,1)} %w_hbm.1, f32[256,512]{1,0:T(8,128)} %f_hbm.1, bf16[256,512]{1,0:T(8,128)(2,1)} %gate_hbm.1, bf16[256,512]{1,0:T(8,128)(2,1)} %cot_hbm.1, ...), custom_call_target="tpu_custom_call" | custom-call | tf_op jit(solution)/shard_map/hyena/pallas_call | solution.py:601
  103.5 0.0 copy-done.1
  103.5 0.0 copy-done
  103.5 2.1 %fusion.1 = (bf16[256,512]{1,0:T(8,128)(2,1)}, bf16[256,512]{1,0:T(8,128)(2,1)}, bf16[256,512]{1,0:T(8,128)(2,1)}) fusion(bf16[256,512]{1,0:T(8,128)(2,1)} %get-tuple-element.6, bf16[256,512]{1,0:T(8,128)(2,1)S(1)} %copy-done.1, bf16[256,512]{1,0:T(8,128)(2,1)S(1)} %copy-done, bf16[256,512]{1,0:T(8,128)(2,1)} %get-tuple-element.8, ...), kind=kLoop, calls=%fused_computation.3 | loop fusion | flops 1441792 | bytes 2097152 | tf_op jit(solution)/shard_map/convert_element_type | solution.py:613
Async XLA Ops:
  0.6 102.9 %copy-start.1 = (bf16[256,512]{1,0:T(8,128)(2,1)S(1)}, bf16[256,512]{1,0:T(8,128)(2,1)}, u32[]{:S(2)}) copy-start(bf16[256,512]{1,0:T(8,128)(2,1)} %cot_hbm.1) | copy-start | bytes 786436
  0.6 102.9 %copy-start = (bf16[256,512]{1,0:T(8,128)(2,1)S(1)}, bf16[256,512]{1,0:T(8,128)(2,1)}, u32[]{:S(2)}) copy-start(bf16[256,512]{1,0:T(8,128)(2,1)} %gate_hbm.1) | copy-start | bytes 786436

commit v3 on v2

--- a/solution.py
+++ b/solution.py
@@ -24,6 +24,7 @@
 ZROWS = HALF * PART
 HW = WIDE // 2
 ORDER = (0, 1, 3, 2)
+FAR_FIRST = (2, 1, 3, 0)
 
 A_FG, A_GV, A_V, A_C = range(4)
 
@@ -105,9 +106,9 @@
             conv_ref, g0_ref, g1_ref,
             x_ref, f_ref, gate_ref, cot_ref, dft_ref, tw_ref, fwd_ref, inv_ref,
             wg, xg, fg, fgr, vt, vr, gvs, gvr, cs, cr,
-            zhi, zlo, spec_f, spec, vacc, dsh, dex, dsum, dy, tz, dz,
+            zs16, spec_f, spec, vacc, dsh, dex, dsum, rl, dy, tz, dz,
             s_a2a, r_a2a, s_gv, s_w, r_w, s_e, r_e, s_xz, r_xz, s_xy, r_xy, s_xc, r_xc,
-            s_dc, r_dc, s_dy, r_dy, s_dz, r_dz, l_in):
+            s_dc, r_dc, s_rl, r_rl, s_dy, r_dy, s_dz, r_dz, l_in):
     i = lax.axis_index("ctx")
     j = lax.axis_index("tp")
     x, zh = i // HN, i % HN
@@ -162,13 +163,10 @@
     fg[:, ROWS:] = jnp.transpose(cot_ref[...].astype(F32) * gate_ref[...].astype(F32)).astype(BF16)
     for load in loads[3:]:
         load.wait()
-    hi = dft_ref[...].astype(BF16)
-    fwd_ref[0] = hi
-    fwd_ref[1] = (dft_ref[...] - hi.astype(F32)).astype(BF16)
+    fwd_ref[...] = dft_ref[...].astype(BF16)
     low, high = slice(0, ROWS), slice(ROWS, WIDE)
-    for n in (0, 1):
-        for rows, cols in ((low, low), (low, high), (high, low), (high, high)):
-            inv_ref[n, rows, cols] = fwd_ref[n, cols, rows] * (1.0 / 4096.0)
+    for rows, cols in ((low, low), (low, high), (high, low), (high, high)):
+        inv_ref[rows, cols] = (dft_ref[cols, rows] * (1.0 / 4096.0)).astype(BF16)
     pl.semaphore_wait(barrier, GROUP - 1 + 3 + 1 + 2)
 
     def spread(kind, k, src_of, dst, own):
@@ -279,15 +277,11 @@
                 if im is None:
                     im = jnp.zeros_like(re)
                 at = slice(k * PART, (k + 1) * PART)
-                for part, off in ((re, 0), (im, ROWS)):
-                    hi = part.astype(BF16)
-                    zhi[at, pl.ds(l0 + off, 128)] = hi
-                    zlo[at, pl.ds(l0 + off, 128)] = (part - hi.astype(F32)).astype(BF16)
+                zs16[at, pl.ds(l0, 128)] = re.astype(BF16)
+                zs16[at, pl.ds(l0 + ROWS, 128)] = im.astype(BF16)
             return carry
         lax.fori_loop(0, 2, step, 0)
-        out[...] = (jnp.dot(zhi[...], fwd_ref[0], preferred_element_type=F32)
-                    + jnp.dot(zlo[...], fwd_ref[0], preferred_element_type=F32)
-                    + jnp.dot(zhi[...], fwd_ref[1], preferred_element_type=F32))
+        out[...] = jnp.dot(zs16[...], fwd_ref[...], preferred_element_type=F32)
 
     def from_spectrum(sign, filt, store):
         def product(n, carry):
@@ -298,15 +292,11 @@
                 re, im = ar * br - ai * bi, ar * bi + ai * br
             else:
                 re, im = ar * br + ai * bi, ai * br - ar * bi
-            for part, cols in ((re, slice(0, ROWS)), (im, slice(ROWS, 2 * ROWS))):
-                hi = part.astype(BF16)
-                zhi[at, cols] = hi
-                zlo[at, cols] = (part - hi.astype(F32)).astype(BF16)
+            zs16[at, :ROWS] = re.astype(BF16)
+            zs16[at, ROWS:] = im.astype(BF16)
             return carry
         lax.fori_loop(0, HALF, product, 0)
-        spec[...] = (jnp.dot(zhi[...], inv_ref[0], preferred_element_type=F32)
-                     + jnp.dot(zlo[...], inv_ref[0], preferred_element_type=F32)
-                     + jnp.dot(zhi[...], inv_ref[1], preferred_element_type=F32))
+        spec[...] = jnp.dot(zs16[...], inv_ref[...], preferred_element_type=F32)
 
         def step(it, carry):
             l0 = pl.multiple_of(it * 128, 128)
@@ -435,16 +425,22 @@
     def dc_copy(t, xx):
         return remote(dsh.at[t, xx], dex.at[xx], s_dc.at[xx], r_dc.at[xx], other)
 
-    def dy_copy(yy, hr):
-        return remote(dsum.at[yy, hr], dy.at[y, hr], s_dy.at[hr, yy], r_dy.at[hr, y], dev(y=yy))
+    far, above, below = (y + 2) % YN, (y + 1) % YN, (y + YN - 1) % YN
+
+    def relay_copy(hr):
+        return remote(dsum.at[far, hr], rl.at[hr], s_rl.at[hr], r_rl.at[hr], up if hr == 0 else down)
+
+    def dy_copy(side, hr):
+        yy, target = (above, up) if side == 0 else (below, down)
+        return remote(dsum.at[yy, hr], dy.at[side, hr], s_dy.at[side, hr], r_dy.at[side, hr], target)
 
     def grad_block(t, o):
-        xx = block_of(o)
+        xx = (y + o) % YN
         grad_term(t, xx)
         pl.when(a != t)(dc_copy(t, xx).start)
 
     def grad_sum(t, o):
-        xx = block_of(o)
+        xx = (y + o) % YN
 
         @pl.when(a == t)
         def _():
@@ -452,24 +448,45 @@
             for hr in (0, 1):
                 cols = slice(hr * ROWS, (hr + 1) * ROWS)
                 dsum[xx, hr] = (dsh[t, xx, :, cols].astype(F32) + dex[xx, :, cols].astype(F32)).astype(BF16)
-                pl.when(xx != y)(dy_copy(xx, hr).start)
+            if o == 2:
+                relay_copy(0).start()
+                relay_copy(1).start()
+            if o == 1:
+                dy_copy(0, 1).start()
+            if o == 3:
+                dy_copy(1, 0).start()
+
+    def grad_blocks(t):
+        for n, o in enumerate(FAR_FIRST):
+            grad_block(t, o)
+            if n:
+                grad_sum(t, FAR_FIRST[n - 1])
+        grad_sum(t, FAR_FIRST[3])
+
+    def grad_relay(t):
+        @pl.when(a == t)
+        def _():
+            for hr, yy in ((0, above), (1, below)):
+                relay_copy(hr).wait_recv()
+                dsum[yy, hr] = (dsum[yy, hr].astype(F32) + rl[hr].astype(F32)).astype(BF16)
+                dy_copy(hr, hr).start()
 
     def dz_copy(hr):
         return remote(tz.at[hr], dz.at[zl], s_dz.at[hr], r_dz.at[zl], dev(zh=2 * pair + hr, zl=zl_s))
 
-    def grad_along_z(hr):
-        total = dsum[y, hr].astype(F32)
-        for o in ORDER[1:]:
-            yy = (y + o) % YN
-            remote(dsum.at[yy, hr], dy.at[yy, hr], s_dy.at[hr, yy], r_dy.at[hr, yy], other).wait_recv()
-        for o in ORDER[1:]:
-            total += dy[(y + o) % YN, hr].astype(F32)
-        tz[hr] = total.astype(BF16)
-        send_if(jnp.logical_not(stays[hr]), dz_copy(hr))
-
-        @pl.when(stays[hr])
+    def grad_along_z(t):
+        @pl.when(a == t)
         def _():
-            dz[zl] = tz[hr]
+            for hr in (0, 1):
+                for side in (hr, 1 - hr):
+                    dy_copy(side, hr).wait_recv()
+                total = dsum[y, hr].astype(F32) + dy[0, hr].astype(F32) + dy[1, hr].astype(F32)
+                tz[hr] = total.astype(BF16)
+                pl.when(jnp.logical_not(stays[hr]))(dz_copy(hr).start)
+
+                @pl.when(stays[hr])
+                def _(hr=hr):
+                    dz[zl] = tz[hr]
 
     def grad_done():
         for zz in (0, 1):
@@ -488,9 +505,9 @@
         ring_start(0, 2, r)
     fg_arrive(0)
     tokens_along_z()
-    fg_arrive(1)
     exchange(0)
     conv_grad(0)
+    fg_arrive(1)
     ring_forward(0, 2)
     conv_grad(1)
     tokens_along_y()
@@ -506,12 +523,9 @@
     tokens_arrive(3, 1)
     for k in (0, 1):
         gv_arrive(k)
-    for n, o in enumerate(ORDER):
+    for o in ORDER:
         ring_arrive(0, 2, o)
-        grad_block(0, o)
-        if n:
-            grad_sum(0, ORDER[n - 1])
-    grad_sum(0, ORDER[3])
+    grad_blocks(0)
     tokens_arrive(2, 0)
     tokens_arrive(2, 1)
     ring_forward(1, 1)
@@ -522,33 +536,35 @@
         ring_arrive(1, 0, o)
         value_term(0, 1, block_of(o), False)
     send_values(0)
+    grad_relay(0)
     for o in ORDER:
         value_term(1, 0, block_of(o), o == 0)
-    for n, o in enumerate(ORDER):
+    for o in ORDER:
         ring_arrive(1, 1, o)
+    grad_blocks(1)
+    for o in ORDER:
         value_term(1, 1, block_of(o), False)
-        if n == 3:
-            send_values(1)
-        grad_block(1, o)
-        if n:
-            grad_sum(1, ORDER[n - 1])
-    grad_sum(1, ORDER[3])
+    send_values(1)
+    grad_along_z(0)
+    grad_relay(1)
     conv_forward(0)
-    grad_along_z(0)
     grad_along_z(1)
     conv_forward(1)
     for k in (0, 1):
         arrive(A_C, k, lambda g: cr.at[chans(k, g)], cs.at[k, 0])
-    conv_ref[...] = jnp.transpose(cr[...].astype(F32)).astype(BF16)
+        cols = slice(k * HW, (k + 1) * HW)
+        conv_ref[:, cols] = jnp.transpose(cr[cols, :].astype(F32)).astype(BF16)
     grad_done()
 
     for wait in pending:
         wait()
     for q in range(4):
         dc_copy(1 - a, q).wait_send()
-    for o in ORDER[1:]:
-        for hr in (0, 1):
-            dy_copy((y + o) % YN, hr).wait_send()
+    for hr in (0, 1):
+        relay_copy(hr).wait_send()
+        dy_copy(0, hr).wait_send()
+        dy_copy(1, hr).wait_send()
+        pl.when(jnp.logical_not(stays[hr]))(dz_copy(hr).wait_send)
 
 
 def per_device(tokens, in_weight, filters, gate, cotangent):
@@ -562,8 +578,8 @@
         vm((ROWS, WIDE), BF16),
         vm((WIDE, WIDE), F32),
         vm((24, WIDE), F32),
-        vm((2, WIDE, WIDE), BF16),
-        vm((2, WIDE, WIDE), BF16),
+        vm((WIDE, WIDE), BF16),
+        vm((WIDE, WIDE), BF16),
         vm((2, XN, WIDE, WIDE), BF16),
         vm((2, YN, WIDE, WIDE), BF16),
         vm((WIDE, 2 * ROWS), BF16),
@@ -575,14 +591,14 @@
         vm((2, GROUP, PART, ROWS), BF16),
         vm((WIDE, ROWS), BF16),
         vm((ZROWS, WIDE), BF16),
-        vm((ZROWS, WIDE), BF16),
         vm((2, ZROWS, WIDE), F32),
         vm((ZROWS, WIDE), F32),
         vm((2, WIDE, HW), F32),
         vm((2, XN, WIDE, WIDE), BF16),
         vm((XN, WIDE, WIDE), BF16),
         vm((YN, 2, WIDE, ROWS), BF16),
-        vm((YN, 2, WIDE, ROWS), BF16),
+        vm((2, WIDE, ROWS), BF16),
+        vm((2, 2, WIDE, ROWS), BF16),
         vm((2, WIDE, ROWS), BF16),
         vm((2, WIDE, ROWS), BF16),
         dma((4, 2, GROUP)), dma((4, 2, GROUP)),
@@ -593,7 +609,8 @@
         dma((2, 3)), dma((2, 4)),
         dma((2, 4)), dma((2, 4)),
         dma((4,)), dma((4,)),
-        dma((2, 4)), dma((2, 4)),
+        dma((2,)), dma((2,)),
+        dma((2, 2)), dma((2, 2)),
         dma((2,)), dma((2,)),
         dma((7,)),
     ]

time: 106 us -> 101 us (0.953)
  the two profiles are of different devices: /device:TPU:192 before, /device:TPU:1 now
where the time goes in v3:
time: 101 us
  Pallas kernels  98.3 us (97%)
  other arithmetic  2.14 us (2%)
    pallas_call x1, Pallas kernels, per_device(): pl.pallas_call(_kernel, out_shape=(block, block, block), in_specs=[pl.Blo...  98.3 us
    convert_element_type x1, other arithmetic, per_device(): grad_gate = (cotangent.astype(F32) * conv).astype(BF16)  2.14 us

profile of v3, /device:TPU:1, one launch (start us, length us, event | category | flops | bytes accessed | tf_op | source)
XLA Modules:
  0.0 101.1 jit_solution(4449423894346757193)
XLA Ops:
  0.6 0.0 copy-start.1
  0.6 0.0 copy-start
  0.7 98.3 %hyena.1 = (bf16[256,512]{1,0:T(8,128)(2,1)}, bf16[256,512]{1,0:T(8,128)(2,1)}, bf16[256,512]{1,0:T(8,128)(2,1)}) custom-call(bf16[256,512]{1,0:T(8,128)(2,1)} %x_hbm.1, bf16[512,512]{1,0:T(8,128)(2,1)} %w_hbm.1, f32[256,512]{1,0:T(8,128)} %f_hbm.1, bf16[256,512]{1,0:T(8,128)(2,1)} %gate_hbm.1, bf16[256,512]{1,0:T(8,128)(2,1)} %cot_hbm.1, ...), custom_call_target="tpu_custom_call" | custom-call | tf_op jit(solution)/shard_map/hyena/pallas_call | solution.py:618
  98.9 0.0 copy-done.1
  98.9 0.0 copy-done
  99.0 2.1 %fusion.1 = (bf16[256,512]{1,0:T(8,128)(2,1)}, bf16[256,512]{1,0:T(8,128)(2,1)}, bf16[256,512]{1,0:T(8,128)(2,1)}) fusion(bf16[256,512]{1,0:T(8,128)(2,1)} %get-tuple-element.6, bf16[256,512]{1,0:T(8,128)(2,1)S(1)} %copy-done.1, bf16[256,512]{1,0:T(8,128)(2,1)S(1)} %copy-done, bf16[256,512]{1,0:T(8,128)(2,1)} %get-tuple-element.8, ...), kind=kLoop, calls=%fused_computation.3 | loop fusion | flops 1441792 | bytes 2097152 | tf_op jit(solution)/shard_map/convert_element_type | solution.py:630
Async XLA Ops:
  0.6 98.3 %copy-start.1 = (bf16[256,512]{1,0:T(8,128)(2,1)S(1)}, bf16[256,512]{1,0:T(8,128)(2,1)}, u32[]{:S(2)}) copy-start(bf16[256,512]{1,0:T(8,128)(2,1)} %cot_hbm.1) | copy-start | bytes 786436
  0.6 98.3 %copy-start = (bf16[256,512]{1,0:T(8,128)(2,1)S(1)}, bf16[256,512]{1,0:T(8,128)(2,1)}, u32[]{:S(2)}) copy-start(bf16[256,512]{1,0:T(8,128)(2,1)} %gate_hbm.1) | copy-start | bytes 786436

commit v4 on v3

--- a/solution.py
+++ b/solution.py
@@ -106,9 +106,9 @@
             conv_ref, g0_ref, g1_ref,
             x_ref, f_ref, gate_ref, cot_ref, dft_ref, tw_ref, fwd_ref, inv_ref,
             wg, xg, fg, fgr, vt, vr, gvs, gvr, cs, cr,
-            zs16, spec_f, spec, vacc, dsh, dex, dsum, rl, dy, tz, dz,
+            zs16, spec_f, spec, vacc, dsh, dex, dsum, rl, dy, tz, zr, dz,
             s_a2a, r_a2a, s_gv, s_w, r_w, s_e, r_e, s_xz, r_xz, s_xy, r_xy, s_xc, r_xc,
-            s_dc, r_dc, s_rl, r_rl, s_dy, r_dy, s_dz, r_dz, l_in):
+            s_dc, r_dc, s_rl, r_rl, s_dy, r_dy, s_zr, r_zr, s_dz, r_dz, l_in):
     i = lax.axis_index("ctx")
     j = lax.axis_index("tp")
     x, zh = i // HN, i % HN
@@ -471,27 +471,55 @@
                 dsum[yy, hr] = (dsum[yy, hr].astype(F32) + rl[hr].astype(F32)).astype(BF16)
                 dy_copy(hr, hr).start()
 
-    def dz_copy(hr):
-        return remote(tz.at[hr], dz.at[zl], s_dz.at[hr], r_dz.at[zl], dev(zh=2 * pair + hr, zl=zl_s))
+    cross = 1 - h
+    gate_chip = zl == cross
+    mate = dev(zl=1 - zl)
+
+    def mate_copy():
+        return remote(tz.at[cross], zr, s_zr.at[0], r_zr.at[0], mate)
+
+    def near_copy():
+        return remote(tz.at[h], dz.at[zl], s_dz.at[0], r_dz.at[zl], mate)
+
+    def cross_copy():
+        return remote(tz.at[cross], dz.at[0], s_dz.at[1], r_dz.at[0], dev(zh=2 * pair + cross, zl=zl_s))
 
     def grad_along_z(t):
         @pl.when(a == t)
         def _():
-            for hr in (0, 1):
-                for side in (hr, 1 - hr):
+            for hr in (cross, h):
+                for side in (0, 1):
                     dy_copy(side, hr).wait_recv()
                 total = dsum[y, hr].astype(F32) + dy[0, hr].astype(F32) + dy[1, hr].astype(F32)
                 tz[hr] = total.astype(BF16)
-                pl.when(jnp.logical_not(stays[hr]))(dz_copy(hr).start)
-
-                @pl.when(stays[hr])
-                def _(hr=hr):
-                    dz[zl] = tz[hr]
+                if hr is cross:
+                    pl.when(jnp.logical_not(gate_chip))(mate_copy().start)
+                else:
+                    pl.when(jnp.logical_not(here))(near_copy().start)
+
+            @pl.when(here)
+            def _():
+                dz[zl] = tz[h]
+
+    def grad_cross(t):
+        @pl.when(a == t)
+        def _():
+            @pl.when(gate_chip)
+            def _():
+                mate_copy().wait_recv()
+                tz[cross] = (tz[cross].astype(F32) + zr[...].astype(F32)).astype(BF16)
+                cross_copy().start()
 
     def grad_done():
-        for zz in (0, 1):
-            wait = remote(tz.at[0], dz.at[zz], s_dz.at[0], r_dz.at[zz], other).wait_recv
-            pl.when(jnp.logical_not(jnp.logical_and(zz == zl, here)))(wait)
+        @pl.when(here)
+        def _():
+            remote(tz.at[0], dz.at[1 - zl], s_dz.at[0], r_dz.at[1 - zl], other).wait_recv()
+
+        @pl.when(jnp.logical_not(here))
+        def _():
+            remote(tz.at[0], dz.at[0], s_dz.at[0], r_dz.at[0], other).wait_recv()
+            dz[1] = jnp.zeros((WIDE, ROWS), BF16)
+
         g0_ref[...] = jnp.transpose(dz[0].astype(F32)).astype(BF16)
         g1_ref[...] = jnp.transpose(dz[1].astype(F32)).astype(BF16)
 
@@ -548,8 +576,10 @@
     grad_along_z(0)
     grad_relay(1)
     conv_forward(0)
+    grad_cross(0)
     grad_along_z(1)
     conv_forward(1)
+    grad_cross(1)
     for k in (0, 1):
         arrive(A_C, k, lambda g: cr.at[chans(k, g)], cs.at[k, 0])
         cols = slice(k * HW, (k + 1) * HW)
@@ -560,11 +590,13 @@
         wait()
     for q in range(4):
         dc_copy(1 - a, q).wait_send()
+    pl.when(jnp.logical_not(here))(near_copy().wait_send)
+    pl.when(jnp.logical_not(gate_chip))(mate_copy().wait_send)
+    pl.when(gate_chip)(cross_copy().wait_send)
     for hr in (0, 1):
         relay_copy(hr).wait_send()
         dy_copy(0, hr).wait_send()
         dy_copy(1, hr).wait_send()
-        pl.when(jnp.logical_not(stays[hr]))(dz_copy(hr).wait_send)
 
 
 def per_device(tokens, in_weight, filters, gate, cotangent):
@@ -600,6 +632,7 @@
         vm((2, WIDE, ROWS), BF16),
         vm((2, 2, WIDE, ROWS), BF16),
         vm((2, WIDE, ROWS), BF16),
+        vm((WIDE, ROWS), BF16),
         vm((2, WIDE, ROWS), BF16),
         dma((4, 2, GROUP)), dma((4, 2, GROUP)),
         dma((2, GROUP)),
@@ -611,6 +644,7 @@
         dma((4,)), dma((4,)),
         dma((2,)), dma((2,)),
         dma((2, 2)), dma((2, 2)),
+        dma((1,)), dma((1,)),
         dma((2,)), dma((2,)),
         dma((7,)),
     ]

time: 101 us -> 101 us (level); the launches traced: 101 us -> 99.3 us
  Pallas kernels: 98.3 us -> 96.5 us
    pallas_call x1, Pallas kernels: 98.3 us -> 96.5 us  [per_device(): pl.pallas_call(_kernel, out_shape=(block, block, block), in_specs=[pl.Blo...]
where the time goes in v4:
time: 101 us; the launch traced here: 99.3 us
  Pallas kernels  96.5 us (96%)
  other arithmetic  2.14 us (2%)
    pallas_call x1, Pallas kernels, per_device(): pl.pallas_call(_kernel, out_shape=(block, block, block), in_specs=[pl.Blo...  96.5 us
    convert_element_type x1, other arithmetic, per_device(): grad_gate = (cotangent.astype(F32) * conv).astype(BF16)  2.14 us

profile of v4, /device:TPU:1, one launch (start us, length us, event | category | flops | bytes accessed | tf_op | source)
XLA Modules:
  0.0 99.3 jit_solution(10526276194498600701)
XLA Ops:
  0.6 0.0 copy-start.1
  0.6 0.0 copy-start
  0.7 96.5 %hyena.1 = (bf16[256,512]{1,0:T(8,128)(2,1)}, bf16[256,512]{1,0:T(8,128)(2,1)}, bf16[256,512]{1,0:T(8,128)(2,1)}) custom-call(bf16[256,512]{1,0:T(8,128)(2,1)} %x_hbm.1, bf16[512,512]{1,0:T(8,128)(2,1)} %w_hbm.1, f32[256,512]{1,0:T(8,128)} %f_hbm.1, bf16[256,512]{1,0:T(8,128)(2,1)} %gate_hbm.1, bf16[256,512]{1,0:T(8,128)(2,1)} %cot_hbm.1, ...), custom_call_target="tpu_custom_call" | custom-call | tf_op jit(solution)/shard_map/hyena/pallas_call | solution.py:652
  97.2 0.0 copy-done.1
  97.2 0.0 copy-done
  97.2 2.1 %fusion.1 = (bf16[256,512]{1,0:T(8,128)(2,1)}, bf16[256,512]{1,0:T(8,128)(2,1)}, bf16[256,512]{1,0:T(8,128)(2,1)}) fusion(bf16[256,512]{1,0:T(8,128)(2,1)} %get-tuple-element.6, bf16[256,512]{1,0:T(8,128)(2,1)S(1)} %copy-done.1, bf16[256,512]{1,0:T(8,128)(2,1)S(1)} %copy-done, bf16[256,512]{1,0:T(8,128)(2,1)} %get-tuple-element.8, ...), kind=kLoop, calls=%fused_computation.3 | loop fusion | flops 1441792 | bytes 2097152 | tf_op jit(solution)/shard_map/convert_element_type | solution.py:664
Async XLA Ops:
  0.6 96.6 %copy-start.1 = (bf16[256,512]{1,0:T(8,128)(2,1)S(1)}, bf16[256,512]{1,0:T(8,128)(2,1)}, u32[]{:S(2)}) copy-start(bf16[256,512]{1,0:T(8,128)(2,1)} %cot_hbm.1) | copy-start | bytes 786436
  0.6 96.6 %copy-start = (bf16[256,512]{1,0:T(8,128)(2,1)S(1)}, bf16[256,512]{1,0:T(8,128)(2,1)}, u32[]{:S(2)}) copy-start(bf16[256,512]{1,0:T(8,128)(2,1)} %gate_hbm.1) | copy-start | bytes 786436

commit v5 on v4

--- a/solution.py
+++ b/solution.py
@@ -584,7 +584,8 @@
         arrive(A_C, k, lambda g: cr.at[chans(k, g)], cs.at[k, 0])
         cols = slice(k * HW, (k + 1) * HW)
         conv_ref[:, cols] = jnp.transpose(cr[cols, :].astype(F32)).astype(BF16)
-    grad_done()
+        if k == 0:
+            grad_done()
 
     for wait in pending:
         wait()

time: 101 us -> 101 us (level)
  no operation moved by 1% of the time
where the time goes in v5:
time: 101 us; the launch traced here: 99.1 us
  Pallas kernels  96.3 us (95%)
  other arithmetic  2.14 us (2%)
    pallas_call x1, Pallas kernels, per_device(): pl.pallas_call(_kernel, out_shape=(block, block, block), in_specs=[pl.Blo...  96.3 us
    convert_element_type x1, other arithmetic, per_device(): grad_gate = (cotangent.astype(F32) * conv).astype(BF16)  2.14 us

profile of v5, /device:TPU:1, one launch (start us, length us, event | category | flops | bytes accessed | tf_op | source)
XLA Modules:
  0.0 99.1 jit_solution(18059704415156805094)
XLA Ops:
  0.6 0.0 copy-start.1
  0.6 0.0 copy-start
  0.7 96.3 %hyena.1 = (bf16[256,512]{1,0:T(8,128)(2,1)}, bf16[256,512]{1,0:T(8,128)(2,1)}, bf16[256,512]{1,0:T(8,128)(2,1)}) custom-call(bf16[256,512]{1,0:T(8,128)(2,1)} %x_hbm.1, bf16[512,512]{1,0:T(8,128)(2,1)} %w_hbm.1, f32[256,512]{1,0:T(8,128)} %f_hbm.1, bf16[256,512]{1,0:T(8,128)(2,1)} %gate_hbm.1, bf16[256,512]{1,0:T(8,128)(2,1)} %cot_hbm.1, ...), custom_call_target="tpu_custom_call" | custom-call | tf_op jit(solution)/shard_map/hyena/pallas_call | solution.py:653
  97.0 0.0 copy-done.1
  97.0 0.0 copy-done
  97.0 2.1 %fusion.1 = (bf16[256,512]{1,0:T(8,128)(2,1)}, bf16[256,512]{1,0:T(8,128)(2,1)}, bf16[256,512]{1,0:T(8,128)(2,1)}) fusion(bf16[256,512]{1,0:T(8,128)(2,1)} %get-tuple-element.6, bf16[256,512]{1,0:T(8,128)(2,1)S(1)} %copy-done.1, bf16[256,512]{1,0:T(8,128)(2,1)S(1)} %copy-done, bf16[256,512]{1,0:T(8,128)(2,1)} %get-tuple-element.8, ...), kind=kLoop, calls=%fused_computation.3 | loop fusion | flops 1441792 | bytes 2097152 | tf_op jit(solution)/shard_map/convert_element_type | solution.py:665
Async XLA Ops:
  0.6 96.3 %copy-start.1 = (bf16[256,512]{1,0:T(8,128)(2,1)S(1)}, bf16[256,512]{1,0:T(8,128)(2,1)}, u32[]{:S(2)}) copy-start(bf16[256,512]{1,0:T(8,128)(2,1)} %cot_hbm.1) | copy-start | bytes 786436
  0.6 96.3 %copy-start = (bf16[256,512]{1,0:T(8,128)(2,1)S(1)}, bf16[256,512]{1,0:T(8,128)(2,1)}, u32[]{:S(2)}) copy-start(bf16[256,512]{1,0:T(8,128)(2,1)} %gate_hbm.1) | copy-start | bytes 786436
